TPU v7x, 32 devices: a whole 2x2x4 slice. The times are simulated.
32 devices in a mesh: row: 8 (over z, y), col: 4 (over x, core).
Axes of the slice: x: 2, y: 2, z: 4, core: 2. Of those that a mesh axis runs over, the one named last changes fastest.
Arguments:
- panels: bfloat16 [16, 32, 128, 128], P('row', 'col'), may hold values from -0.26367188 to 0.26367188
- obs_of: int32 [16, 32], replicated, may hold values from 0 to 63, as said below
- counts: int32 [16], replicated, may hold values from 16 to 32, as said below
- inv_var: float32 [64, 128], replicated, may hold values from 0.25 to 4
- pattern: int32 [16, 16], replicated, may hold values from 0 to 1, as said below
- prior: float32 [2048, 2048], P('row', 'col'), may hold values from -2 to 2
Outputs:
- information: float32 [2048, 2048], P('row', 'col')
Inputs may be any that keep to these rules, and one draw needn't show every extreme that they name: The 32 entries of a row of obs_of are distinct. `counts`: some panel has all 32 slots live. pattern is 1 on the diagonal and 0 below it.
All inputs are finite; a program needn't handle non-finite values.
Results may differ from a plain program's by a relative error of at most 0.0011.
Values may be sent and summed in bfloat16 or wider, within the bound.
A program may use at most 64 MiB of HBM per device.

v0:
```python
import jax
import jax.numpy as jnp
from jax import lax
from jax.sharding import PartitionSpec as P


def on_device(panels, obs_of, counts, inv_var, pattern, prior):
    row_count = lax.axis_size("row")
    col_count = lax.axis_size("col")
    row_index = lax.axis_index("row")
    col_index = lax.axis_index("col")
    group_rows = panels.shape[0]
    share_slots = panels.shape[1]
    block_size = panels.shape[2]
    fold_ratio = row_count // col_count
    group_cols = group_rows * fold_ratio
    slot_count = obs_of.shape[1]
    row_start = row_index * group_rows
    col_start = col_index * group_cols
    slot_ids = jnp.arange(slot_count, dtype=jnp.int32)
    own_ids = lax.dynamic_slice(
        obs_of, (row_start, col_index * share_slots), (group_rows, share_slots)
    )
    own_counts = lax.dynamic_slice_in_dim(counts, row_start, group_rows, 0)
    own_slots = col_index * share_slots + jnp.arange(share_slots, dtype=jnp.int32)
    own_live = (own_slots[None, :] < own_counts[:, None]).astype(jnp.float32)
    root_weight = jnp.sqrt(jnp.take(inv_var, own_ids, axis=0)) * own_live[:, :, None]
    scaled = (panels.astype(jnp.float32) * root_weight[:, :, :, None]).astype(jnp.bfloat16)
    row_panels = lax.all_gather(scaled, "col", axis=1, tiled=True)
    every_row = lax.all_gather(scaled, "row", axis=0, tiled=True)
    col_panels = lax.all_to_all(every_row, "col", split_axis=0, concat_axis=1, tiled=True)
    row_ids = lax.dynamic_slice_in_dim(obs_of, row_start, group_rows, 0)
    col_ids = lax.dynamic_slice_in_dim(obs_of, col_start, group_cols, 0)
    same_obs = row_ids[:, :, None, None] == col_ids[None, None, :, :]
    has_match = jnp.any(same_obs, axis=3)
    partner = jnp.sum(jnp.where(same_obs, slot_ids[None, None, None, :], 0), axis=3)
    col_pick = jnp.arange(group_cols, dtype=jnp.int32)[None, :]

    def compute_tile(unused):
        rows_done = []
        for local_row in range(group_rows):
            aligned = col_panels[col_pick, partner[local_row]]
            aligned = jnp.where(
                has_match[local_row][:, :, None, None], aligned, jnp.zeros((), jnp.bfloat16)
            )
            rows_done.append(
                jnp.einsum(
                    "pax,pjay->jxy",
                    row_panels[local_row],
                    aligned,
                    preferred_element_type=jnp.float32,
                )
            )
        return jnp.stack(rows_done, 0)

    def zero_tile(unused):
        return jnp.zeros((group_rows, group_cols, block_size, block_size), jnp.float32)

    block_rows = row_start + jnp.arange(group_rows, dtype=jnp.int32)
    block_cols = col_start + jnp.arange(group_cols, dtype=jnp.int32)
    upper_mask = block_rows[:, None] <= block_cols[None, :]
    tile_pattern = lax.dynamic_slice(pattern, (row_start, col_start), (group_rows, group_cols))
    kept_blocks = upper_mask & (tile_pattern == 1)
    needed = jnp.any(upper_mask)
    product = lax.cond(needed, compute_tile, zero_tile, 0)
    own_part = jnp.where(kept_blocks[:, :, None, None], product, 0.0)
    strict_mask = (block_rows[:, None] < block_cols[None, :])[:, :, None, None]
    strict_part = jnp.where(strict_mask, own_part, 0.0)
    piece_rows = block_size // col_count
    outgoing = strict_part.reshape(group_rows, fold_ratio, group_rows, block_size, block_size)
    outgoing = jnp.transpose(outgoing, (1, 2, 0, 4, 3))
    outgoing = outgoing.reshape(
        1, fold_ratio, group_rows, group_rows, col_count, piece_rows, block_size
    )
    section_one = lax.all_to_all(outgoing, "col", split_axis=4, concat_axis=0, tiled=True)
    section_one = section_one.reshape(
        1, col_count * fold_ratio, group_rows, group_rows, piece_rows, block_size
    )
    section_two = lax.all_to_all(section_one, "row", split_axis=1, concat_axis=0, tiled=True)
    section_two = section_two.reshape(
        1, col_count, fold_ratio, group_rows, group_rows, piece_rows, block_size
    )
    section_three = lax.all_to_all(section_two, "col", split_axis=1, concat_axis=0, tiled=True)
    section_three = section_three.reshape(
        col_count, fold_ratio, group_rows, group_rows, piece_rows, block_size
    )
    mirrored = jnp.transpose(section_three, (2, 1, 3, 0, 4, 5)).reshape(
        group_rows, group_cols, block_size, block_size
    )
    update = own_part + mirrored
    tile_update = jnp.transpose(update, (0, 2, 1, 3)).reshape(
        group_rows * block_size, group_cols * block_size
    )
    return prior + tile_update


def solution(mesh):
    placed = (P("row", "col", None, None), P(), P(), P(), P(), P("row", "col"))
    return jax.shard_map(
        on_device, mesh=mesh, in_specs=placed, out_specs=P("row", "col"), check_vma=False
    )
```

profile of v0, /device:TPU:24, one launch (start us, length us, event | category | flops | bytes accessed | tf_op | source)
XLA Modules:
  0.0 227.7 jit_solution(14949335172750620274)
XLA Ops:
  7.4 0.7 dynamic_slice.25
  8.1 0.8 compare_and_fusion.1
  8.9 0.1 reshape.197
  9.0 0.6 gather_fusion.2
  9.5 0.1 fusion.34
  9.6 2.2 multiply_convert_fusion
  11.8 0.0 all-gather.3.cloned.1.call-update
  11.8 72.8 %all-gather.3.cloned.1.call-done = bf16[16,8,128,128]{3,2,1,0:T(8,128)(2,1)} async-done(((bf16[2,8,128,128]{3,2,1,0:T(8,128)(2,1)}), bf16[16,8,128,128]{3,2,1,0:T(8,128)(2,1)}) %all-gather.3.cloned.1.call-update) | async-done | bytes 4194320 | tf_op jit(solution)/shard_map/all_gather | solution.py:30
  84.6 4.8 %all-to-all-start = ((bf16[16,8,128,128]{3,2,1,0:T(8,128)(2,1)}), bf16[16,8,128,128]{3,2,1,0:T(8,128)(2,1)}, u32[]{:S(2)}, u32[]{:S(2)}) async-start(bf16[16,8,128,128]{3,2,1,0:T(8,128)(2,1)} %all-gather.3.cloned.1.call-done), calls=%async_computation | async-start | bytes 8388608 | tf_op jit(solution)/shard_map/all_to_all | solution.py:31
  89.4 0.0 all-gather.5.cloned.1.call-start
  89.5 0.5 all-gather.5.cloned.1.call-update
  90.0 1.4 compare_and_fusion
  91.9 56.9 %all-to-all-done = bf16[16,8,128,128]{3,2,1,0:T(8,128)(2,1)} async-done(((bf16[16,8,128,128]{3,2,1,0:T(8,128)(2,1)}), bf16[16,8,128,128]{3,2,1,0:T(8,128)(2,1)}, u32[]{:S(2)}, u32[]{:S(2)}) %all-to-all-start) | async-done | bytes 4194336 | tf_op jit(solution)/shard_map/all_to_all | solution.py:31
  148.9 4.7 %copy.61 = bf16[4,4,8,128,128]{4,3,2,0,1:T(8,128)(2,1)} copy(bf16[4,4,8,128,128]{4,3,2,1,0:T(8,128)(2,1)} %bitcast.22) | data formatting | bytes 8388608 | tf_op jit(solution)/shard_map/all_to_all | solution.py:31
  153.6 0.1 conditional.1
  153.7 0.1 select_select_fusion
  153.8 0.2 copy.44
  154.0 0.0 copy-start.1
  154.1 35.6 %all_to_all.52 = f32[1,2,2,2,4,32,128]{6,5,3,2,1,0,4:T(8,128)S(1)} all-to-all(f32[1,2,2,2,4,32,128]{6,5,3,2,1,0,4:T(8,128)S(1)} %copy.45), channel_id=1, replica_groups=mesh['row'=8,'col'=4] {'col'}, dimensions={4} | all-to-all | bytes 1048576 | tf_op jit(solution)/shard_map/all_to_all | solution.py:75
  189.7 17.9 %all_to_all.53 = f32[1,8,2,2,32,128]{5,4,3,2,0,1:T(8,128)S(1)} all-to-all(f32[1,8,2,2,32,128]{5,4,3,2,0,1:T(8,128)S(1)} %bitcast.87), channel_id=1, replica_groups=mesh['row'=8,'col'=4] {'row'}, dimensions={1} | all-to-all | bytes 1048576 | tf_op jit(solution)/shard_map/all_to_all | solution.py:79
  207.6 11.2 %all_to_all.54 = f32[1,4,2,2,2,32,128]{6,5,4,3,2,0,1:T(8,128)S(1)} all-to-all(f32[1,4,2,2,2,32,128]{6,5,4,3,2,0,1:T(8,128)S(1)} %bitcast.88), channel_id=1, replica_groups=mesh['row'=8,'col'=4] {'col'}, dimensions={1} | all-to-all | bytes 1048576 | tf_op jit(solution)/shard_map/all_to_all | solution.py:83
  218.9 0.1 add_bitcast_fusion
  219.0 0.3 copy.49
  219.4 0.9 bitcast_add_fusion
  (14 shorter events, 0.2 us)
Async XLA Ops:
  7.4 1.6 copy-start
  7.4 77.2 %all-gather.3.cloned.1.call-start = ((), (), s32[]{:S(2)}) async-start(), calls=%async_computation.4 | async-start | bytes 4718592 | tf_op jit(solution)/shard_map/all_gather | solution.py:30
  84.6 64.3 %all-to-all-start = ((bf16[16,8,128,128]{3,2,1,0:T(8,128)(2,1)}), bf16[16,8,128,128]{3,2,1,0:T(8,128)(2,1)}, u32[]{:S(2)}, u32[]{:S(2)}) async-start(bf16[16,8,128,128]{3,2,1,0:T(8,128)(2,1)} %all-gather.3.cloned.1.call-done), calls=%async_computation | async-start | bytes 8388608 | tf_op jit(solution)/shard_map/all_to_all | solution.py:31
  89.4 64.2 %all-gather.5.cloned.1.call-start = ((), (), s32[]{:S(2)}) async-start(), calls=%async_computation.5 | async-start | bytes 2621440 | tf_op jit(solution)/shard_map/all_gather | solution.py:29
  154.0 65.4 %copy-start.1 = (f32[256,512]{1,0:T(8,128)S(1)}, f32[256,512]{1,0:T(8,128)}, u32[]{:S(2)}) copy-start(f32[256,512]{1,0:T(8,128)} %param.13) | copy-start | bytes 1572868
Sparse Core Ops, SparseCore 0:
  11.9 72.6 all-gather.2
Sparse Core Ops, SparseCore 1:
  91.5 34.3 all-gather.4
where the time goes:
time: 232 us; the launch traced here: 228 us
  waiting for transfers between devices  130 us (56%)
  blocking collectives  64.8 us (28%)
  between operations  15.5 us (7%)
  local copies, waits for them, and re-layouts  6.77 us (3%)
  other arithmetic  5.53 us (2%)
  starting transfers between devices  4.88 us (2%)
    all_gather x1, waiting for transfers between devices, on_device(): every_row = lax.all_gather(scaled, 'row', axis=0, tiled=True)  72.8 us
    all_to_all x1, waiting for transfers between devices, on_device(): lax.all_to_all(every_row, 'col', split_axis=0, concat_axis=1, tiled=True)  56.9 us
    all_to_all x1, blocking collectives, on_device(): lax.all_to_all(outgoing, 'col', split_axis=4, concat_axis=0, tiled=True)  35.6 us
    all_to_all x1, blocking collectives, on_device(): lax.all_to_all(section_one, 'row', split_axis=1, concat_axis=0, tiled=True)  17.9 us
    all_to_all x1, blocking collectives, on_device(): lax.all_to_all(section_two, 'col', split_axis=1, concat_axis=0, tiled=True)  11.2 us
    all_to_all x1, starting transfers between devices, on_device(): lax.all_to_all(every_row, 'col', split_axis=0, concat_axis=1, tiled=True)  4.83 us
    all_to_all x1, local copies, waits for them, and re-layouts, on_device(): lax.all_to_all(every_row, 'col', split_axis=0, concat_axis=1, tiled=True)  4.71 us
  transfers between devices with their start and end apart: 3, of which 2 were waited for; matrix products, arithmetic and copies ran while one was open for 3% of the time, Pallas kernels for 0%

commit v1 on v0

v1 whole, which is shorter than its diff:
```python
import functools

import jax
import jax.numpy as jnp
from jax import lax
from jax.experimental import pallas as pl
from jax.experimental.pallas import tpu as pltpu
from jax.sharding import PartitionSpec as P

MESH = pl.DeviceIdType.MESH


def gather_kernel(planes, fold, obs_ref, counts_ref, var_ref, panels_ref, rows_ref, cols_ref,
                  held, turned, z_send, z_recv, x_send, x_recv, y_send, y_recv, r_send, r_recv, keep):
    row, col = lax.axis_index("row"), lax.axis_index("col")
    plane, part = row // fold, row % fold
    groups, share = panels_ref.shape[0], panels_ref.shape[1]

    def at(other_row, other_col):
        return {"row": other_row, "col": other_col}

    def other_plane(step):
        return lax.rem(plane + step, planes)

    def other_col(step):
        return lax.rem(col + step, planes)

    def other_part(step):
        return lax.rem(part + step, fold)

    partners = [at(other_plane(s) * fold + part, col) for s in range(1, planes)]
    partners += [at(row, other_col(s)) for s in range(1, planes)]
    partners += [at(plane * fold + other_part(s), col) for s in range(1, fold)]
    barrier = pltpu.get_barrier_semaphore()
    for partner in partners:
        pl.semaphore_signal(barrier, inc=1, device_id=partner, device_id_type=MESH)

    weights = []
    for g in range(groups):
        block = row * groups + g
        for p in range(share):
            slot = col * share + p
            live = jnp.where(slot < counts_ref[block], 1.0, 0.0)
            weights.append(jnp.sqrt(var_ref[pl.ds(obs_ref[block, slot], 1), :]) * live)
    weights = jnp.concatenate(weights, axis=0).T
    for g in range(groups):
        for p in range(share):
            j = g * share + p
            scaled = panels_ref[g, p].astype(jnp.float32) * weights[:, j:j + 1]
            held[plane, g, p] = scaled.astype(jnp.bfloat16)
            turned[g, p] = scaled.T.astype(jnp.bfloat16)

    pl.semaphore_wait(barrier, len(partners))

    def z_copy(step, g, landing):
        return pltpu.make_async_remote_copy(
            src_ref=held.at[landing, g], dst_ref=held.at[landing, g],
            send_sem=z_send.at[step - 1, g], recv_sem=z_recv.at[landing, g],
            device_id=at(other_plane(step) * fold + part, col), device_id_type=MESH)

    def r_copy(step, landing):
        return pltpu.make_async_remote_copy(
            src_ref=turned, dst_ref=rows_ref.at[landing],
            send_sem=r_send.at[step - 1], recv_sem=r_recv.at[landing],
            device_id=at(row, other_col(step)), device_id_type=MESH)

    def x_copy(from_plane, g, landing):
        return pltpu.make_async_remote_copy(
            src_ref=held.at[from_plane, g], dst_ref=cols_ref.at[part, landing, g],
            send_sem=x_send.at[from_plane, g], recv_sem=x_recv.at[landing, g],
            device_id=at(row, from_plane), device_id_type=MESH)

    def y_copy(step, slot, g, landing):
        return pltpu.make_async_remote_copy(
            src_ref=cols_ref.at[landing, slot, g], dst_ref=cols_ref.at[landing, slot, g],
            send_sem=y_send.at[step - 1, slot, g], recv_sem=y_recv.at[landing, slot, g],
            device_id=at(plane * fold + other_part(step), col), device_id_type=MESH)

    def keep_copy(g):
        return pltpu.make_async_copy(held.at[col, g], cols_ref.at[part, col, g], keep.at[g])

    order = sorted(range(1, planes), key=lambda s: -min(s, planes - s))
    order = list(range(1, planes))
    for step in order:
        for g in range(groups):
            z_copy(step, g, plane).start()
    own_row = pltpu.make_async_copy(turned, rows_ref.at[col], keep.at[groups])
    own_row.start()

    def spread(from_plane):
        for g in range(groups):
            @pl.when(from_plane != col)
            def _():
                x_copy(from_plane, g, col).start()

            @pl.when(from_plane == col)
            def _():
                keep_copy(g).start()

    def forward(from_plane):
        @pl.when(from_plane == col)
        def _():
            for g in range(groups):
                keep_copy(g).wait()
                for step in range(1, fold):
                    y_copy(step, col, g, part).start()
            for s in range(1, planes):
                for g in range(groups):
                    x_copy(col, g, other_col(s)).wait_recv()
                    for step in range(1, fold):
                        y_copy(step, other_col(s), g, part).start()

    spread(plane)
    for step in range(1, planes):
        r_copy(step, col).start()
    before = plane
    for step in order:
        here = other_plane(step)
        for g in range(groups):
            z_copy(step, g, here).wait_recv()
        spread(here)
        forward(before)
        before = here
    forward(before)

    for step in range(1, planes):
        r_copy(step, other_col(step)).wait_recv()
    for step in range(1, fold):
        for slot in range(planes):
            for g in range(groups):
                y_copy(step, slot, g, other_part(step)).wait_recv()
    own_row.wait()
    for step in range(1, planes):
        r_copy(step, col).wait_send()
        for g in range(groups):
            z_copy(step, g, plane).wait_send()
            x_copy(other_col(step), g, col).wait_send()
    for step in range(1, fold):
        for slot in range(planes):
            for g in range(groups):
                y_copy(step, slot, g, part).wait_send()


def product_kernel(fold, width, place_ref, pattern_ref, rows_ref, cols_ref, prior_ref, out_ref, total):
    row, col = lax.axis_index("row"), lax.axis_index("col")
    groups, share, size = rows_ref.shape[1], rows_ref.shape[2], rows_ref.shape[3]
    block_cols = groups * fold
    observations = place_ref.shape[1]
    total[...] = jnp.zeros_like(total)
    zero = jnp.zeros((size, size), jnp.bfloat16)

    def step(i, unused):
        left, right = [], []
        for k in range(width):
            obs = i * width + k
            tiles = []
            for g in range(groups):
                slot = place_ref[row * groups + g, obs]
                safe = jnp.maximum(slot, 0)
                tile = rows_ref[safe // share, g, safe % share]
                tiles.append(jnp.where(slot >= 0, tile, zero))
            left.append(jnp.concatenate(tiles, axis=0))
            tiles = []
            for j in range(block_cols):
                slot = place_ref[col * block_cols + j, obs]
                safe = jnp.maximum(slot, 0)
                tile = cols_ref[j // groups, safe // share, j % groups, safe % share]
                tiles.append(jnp.where(slot >= 0, tile, zero))
            right.append(jnp.concatenate(tiles, axis=1))
        total[...] += jnp.dot(jnp.concatenate(left, axis=1), jnp.concatenate(right, axis=0),
                              preferred_element_type=jnp.float32)
        return unused

    lax.fori_loop(0, observations // width, step, 0)
    for g in range(groups):
        for j in range(block_cols):
            a, b = row * groups + g, col * block_cols + j
            kept = pattern_ref[jnp.minimum(a, b), jnp.maximum(a, b)] == 1
            across, down = pl.ds(g * size, size), pl.ds(j * size, size)
            out_ref[across, down] = prior_ref[across, down] + jnp.where(
                kept, total[across, down], 0.0)


def on_device(panels, obs_of, counts, inv_var, pattern, prior):
    planes = lax.axis_size("col")
    fold = lax.axis_size("row") // planes
    groups, share, size, _ = panels.shape
    observations = inv_var.shape[0]
    slots = jnp.arange(obs_of.shape[1], dtype=jnp.int32)
    found = obs_of[:, None, :] == jnp.arange(observations, dtype=jnp.int32)[None, :, None]
    place = jnp.max(jnp.where(found, slots[None, None, :], -1), axis=2)
    smem = pl.BlockSpec(memory_space=pltpu.SMEM)
    vmem = pl.BlockSpec(memory_space=pltpu.VMEM)
    dma = pltpu.SemaphoreType.DMA
    rows, cols = pl.pallas_call(
        functools.partial(gather_kernel, planes, fold),
        out_shape=(jax.ShapeDtypeStruct((planes, groups, share, size, size), jnp.bfloat16),
                   jax.ShapeDtypeStruct((fold, planes, groups, share, size, size), jnp.bfloat16)),
        in_specs=[smem, smem, vmem, vmem],
        out_specs=(vmem, vmem),
        scratch_shapes=[
            pltpu.VMEM((planes, groups, share, size, size), jnp.bfloat16),
            pltpu.VMEM((groups, share, size, size), jnp.bfloat16),
            dma((planes - 1, groups)), dma((planes, groups)),
            dma((planes, groups)), dma((planes, groups)),
            dma((max(fold - 1, 1), planes, groups)), dma((fold, planes, groups)),
            dma((planes - 1,)), dma((planes,)),
            dma((groups + 1,)),
        ],
        compiler_params=pltpu.CompilerParams(
            collective_id=0, has_side_effects=True, vmem_limit_bytes=48 * 1024 * 1024),
    )(obs_of, counts, inv_var, panels)
    return pl.pallas_call(
        functools.partial(product_kernel, fold, 4),
        out_shape=jax.ShapeDtypeStruct(prior.shape, prior.dtype),
        in_specs=[smem, smem, vmem, vmem, vmem],
        out_specs=vmem,
        scratch_shapes=[pltpu.VMEM(prior.shape, jnp.float32)],
        compiler_params=pltpu.CompilerParams(vmem_limit_bytes=48 * 1024 * 1024),
    )(place, pattern, rows, cols, prior)


def solution(mesh):
    placed = (P("row", "col", None, None), P(), P(), P(), P(), P("row", "col"))
    return jax.shard_map(
        on_device, mesh=mesh, in_specs=placed, out_specs=P("row", "col"), check_vma=False
    )
```

time: 232 us -> 114 us (0.49); the launches traced: 228 us -> 113 us
  waiting for transfers between devices: 130 us -> 0 us
  Pallas kernels: 0 us -> 107 us
  blocking collectives: 64.8 us -> 0 us
  between operations: 15.5 us -> 0.04 us
  starting transfers between devices: 4.88 us -> 0 us
  other arithmetic: 5.53 us -> 0.85 us
    pallas_call x0 -> x2, Pallas kernels: none -> 107 us  [the longest x1 97.9 us: on_device(): pl.pallas_call(functools.partial(gather_kernel, planes, fold), out_shape=...]
    all_gather x2 -> x0, waiting for transfers between devices: 72.8 us -> none  [the longest x1 72.8 us: on_device(): every_row = lax.all_gather(scaled, 'row', axis=0, tiled=True)]
    all_to_all x3 -> x0, blocking collectives: 64.8 us -> none  [the longest x1 35.6 us: on_device(): lax.all_to_all(outgoing, 'col', split_axis=4, concat_axis=0, tiled=True)]
    all_to_all x1 -> x0, waiting for transfers between devices: 56.9 us -> none  [on_device(): lax.all_to_all(every_row, 'col', split_axis=0, concat_axis=1, tiled=True)]
    unnamed x4 -> x12, local copies, waits for them, and re-layouts: 0.01 us -> 4.88 us
    all_to_all x1 -> x0, starting transfers between devices: 4.83 us -> none  [on_device(): lax.all_to_all(every_row, 'col', split_axis=0, concat_axis=1, tiled=True)]
    all_to_all x2 -> x0, local copies, waits for them, and re-layouts: 4.74 us -> none  [the longest x1 4.71 us: on_device(): lax.all_to_all(every_row, 'col', split_axis=0, concat_axis=1, tiled=True)]
  transfers between devices with their start and end apart: 3 -> 0, of which waited for: 2 -> 0; matrix products, arithmetic and copies ran while one was open for 3% -> 0% of each run, Pallas kernels for 0% -> 0%
where the time goes in v1:
time: 114 us; the launch traced here: 113 us
  Pallas kernels  107 us (94%)
  local copies, waits for them, and re-layouts  4.88 us (4%)
    pallas_call x1, Pallas kernels, on_device(): pl.pallas_call(functools.partial(gather_kernel, planes, fold), out_shape=...  97.9 us
    pallas_call x1, Pallas kernels, on_device(): pl.pallas_call(functools.partial(product_kernel, fold, 4), out_shape=jax....  9.04 us
    unnamed x12, local copies, waits for them, and re-layouts  4.88 us

profile of v1, /device:TPU:24, one launch (start us, length us, event | category | flops | bytes accessed | tf_op | source)
XLA Modules:
  0.0 112.7 jit_solution(15817752668692480473)
XLA Ops:
  0.0 0.9 select_reduce_fusion.place_ref
  0.9 0.0 copy-start.1
  0.9 1.0 copy-done.1
  1.9 0.0 copy-start.2
  1.9 0.7 copy-done.2
  2.6 0.0 copy-start.3
  2.6 0.8 copy-done.3
  3.4 0.0 copy-start.5
  3.4 0.7 copy-done.5
  4.0 97.9 %shard_map.64 = (bf16[4,2,8,128,128]{4,3,2,1,0:T(8,128)(2,1)S(1)}, bf16[2,4,2,8,128,128]{5,4,3,2,1,0:T(8,128)(2,1)}) custom-call(s32[16,32]{1,0:T(8,128)S(1)} %copy-done.2, s32[16]{0:T(128)S(1)} %copy-done.5, f32[64,128]{1,0:T(8,128)S(1)} %copy-done.3, bf16[2,8,128,128]{3,2,1,0:T(8,128)(2,1)S(1)} %copy-done.1), custom_call_target="tpu_custom_call" | custom-call | tf_op jit(solution)/shard_map/pallas_call | solution.py:195
  101.9 0.0 copy-start
  101.9 1.0 copy-done
  102.9 0.0 copy-start.4
  102.9 0.7 copy-done.4
  103.6 9.0 %shard_map.65 = f32[256,512]{1,0:T(8,128)} custom-call(s32[16,64]{1,0:T(8,128)S(1)} %select_reduce_fusion.place_ref, s32[16,16]{1,0:T(8,128)S(1)} %copy-done.4, bf16[4,2,8,128,128]{4,3,2,1,0:T(8,128)(2,1)S(1)} %get-tuple-element.7.rows_ref, bf16[2,4,2,8,128,128]{5,4,3,2,1,0:T(8,128)(2,1)} %get-tuple-element.8.cols_ref, f32[256,512]{1,0:T(8,128)S(1)} %copy-done), custom_call_target="tpu_custom_call" | custom-call | tf_op jit(solution)/shard_map/pallas_call | solution.py:213
Async XLA Ops:
  0.9 1.0 copy-start.1
  1.9 0.7 copy-start.2
  2.6 0.8 copy-start.3
  3.4 0.7 copy-start.5
  101.9 1.0 copy-start
  102.9 0.7 copy-start.4

commit v2 on v0

v2 whole, which is shorter than its diff:
```python
import functools

import jax
import jax.numpy as jnp
from jax import lax
from jax.experimental import pallas as pl
from jax.experimental.pallas import tpu as pltpu
from jax.sharding import PartitionSpec as P

MESH = pl.DeviceIdType.MESH


def kernel(planes, fold, obs_ref, counts_ref, place_ref, pattern_ref, var_ref, panels_ref, prior_ref, out_ref,
           weights, leaving, held, turned, rows, cols, total, inbox,
           y_send, y_recv, z_send, z_recv, x_send, x_recv, r_send, r_recv, n_send, n_recv,
           t_send, t_recv, keep):
    row, col = lax.axis_index("row"), lax.axis_index("col")
    plane, part = row // fold, row % fold
    groups, share, size = panels_ref.shape[0], panels_ref.shape[1], panels_ref.shape[2]
    depth = size // fold
    wide = share * depth
    near = col + 1 - 2 * lax.rem(col, 2)
    far_steps = range(2, planes, 2)

    def at(other_row, other_col):
        return {"row": other_row, "col": other_col}

    def other_plane(step):
        return lax.rem(plane + step, planes)

    def other_col(step):
        return lax.rem(col + step, planes)

    def other_part(step):
        return lax.rem(part + step, fold)

    partners = [at(other_plane(s) * fold + part, col) for s in (1, planes - 1)]
    partners += [at(row, other_col(s)) for s in range(1, planes)]
    partners += [at(plane * fold + other_part(s), col) for s in range(1, fold)]
    barrier = pltpu.get_barrier_semaphore()
    for partner in partners:
        pl.semaphore_signal(barrier, inc=1, device_id=partner, device_id_type=MESH)

    factors = []
    for g in range(groups):
        block = row * groups + g
        for p in range(share):
            slot = col * share + p
            live = jnp.where(slot < counts_ref[block], 1.0, 0.0)
            factors.append(jnp.sqrt(var_ref[pl.ds(obs_ref[block, slot], 1), :]) * live)
    weights[...] = jnp.concatenate(factors, axis=0).T

    def scaled(to_part, g, p):
        j = g * share + p
        lines = pl.ds(pl.multiple_of(to_part * depth, depth), depth)
        value = panels_ref[g, p, lines, :].astype(jnp.float32) * weights[lines, j:j + 1]
        return value.astype(jnp.bfloat16)

    def copy(src, dst, send, recv, device):
        return pltpu.make_async_remote_copy(
            src_ref=src, dst_ref=dst, send_sem=send, recv_sem=recv,
            device_id=device, device_id_type=MESH)

    def y_copy(step, landing):
        return copy(leaving.at[step - 1], held.at[plane, landing], y_send.at[step - 1],
                    y_recv.at[landing], at(plane * fold + other_part(step), col))

    def z_copy(way, from_plane, chunk):
        target = lax.rem(plane + (1 if way == 0 else planes - 1), planes)
        return copy(held.at[from_plane, chunk], held.at[from_plane, chunk], z_send.at[way, from_plane, chunk],
                    z_recv.at[from_plane, chunk], at(target * fold + part, col))

    def x_copy(to_col, chunk, landing):
        return copy(held.at[to_col, chunk], cols.at[landing, chunk], x_send.at[to_col, chunk],
                    x_recv.at[landing, chunk], at(row, to_col))

    def keep_copy(chunk):
        return pltpu.make_async_copy(held.at[col, chunk], cols.at[col, chunk], keep.at[chunk])

    def far_copy(step, landing):
        return copy(turned, rows.at[landing], r_send.at[step], r_recv.at[landing], at(row, other_col(step)))

    def near_copy(slot, index, landing):
        source = turned if index == 0 else rows.at[slot]
        return copy(source, rows.at[landing], n_send.at[index], n_recv.at[index], at(row, near))

    def t_copy(step, g):
        return copy(total.at[other_part(step), g], inbox.at[step - 1, g], t_send.at[step - 1, g],
                    t_recv.at[step - 1, g], at(plane * fold + other_part(step), col))

    def spread(from_plane, chunk):
        @pl.when(from_plane != col)
        def _():
            x_copy(from_plane, chunk, col).start()

        @pl.when(from_plane == col)
        def _():
            keep_copy(chunk).start()

    def begin(chunk):
        @pl.when(plane < planes - 1)
        def _():
            z_copy(0, plane, chunk).start()

        @pl.when(plane > 0)
        def _():
            z_copy(1, plane, chunk).start()

        spread(plane, chunk)

    def turn(chunk):
        for g in range(groups):
            turned[chunk, g] = held[plane, chunk, g].reshape(wide, size).T

    for step in range(1, fold):
        for g in range(groups):
            for p in range(share):
                leaving[step - 1, g, p] = scaled(other_part(step), g, p)
    pl.semaphore_wait(barrier, len(partners))
    for step in range(1, fold):
        y_copy(step, part).start()
    for g in range(groups):
        for p in range(share):
            held[plane, part, g, p] = scaled(part, g, p)
    begin(part)
    turn(part)
    for step in range(1, fold):
        y_copy(step, other_part(step)).wait_recv()
        begin(other_part(step))
        turn(other_part(step))
    own_row = pltpu.make_async_copy(turned, rows.at[col], keep.at[fold])
    own_row.start()
    near_copy(col, 0, col).start()
    for step in far_steps:
        far_copy(step, col).start()

    def pass_rows():
        for index, step in enumerate(far_steps):
            slot = other_col(step)
            far_copy(step, slot).wait_recv()
            near_copy(slot, index + 1, slot).start()

    for step in range(1, planes):
        for order in range(fold):
            chunk = other_part(order)
            below, above = plane - step, plane + step

            @pl.when(below >= 0)
            def _():
                z_copy(0, below, chunk).wait_recv()

                @pl.when(plane < planes - 1)
                def _():
                    z_copy(0, below, chunk).start()

                spread(below, chunk)

            @pl.when(above < planes)
            def _():
                z_copy(1, above, chunk).wait_recv()

                @pl.when(plane > 0)
                def _():
                    z_copy(1, above, chunk).start()

                spread(above, chunk)
        if step == min(2, planes - 1):
            pass_rows()

    own_row.wait()
    near_copy(near, 0, near).wait_recv()
    for index, step in enumerate(far_steps):
        slot = lax.rem(near + step, planes)
        near_copy(slot, index + 1, slot).wait_recv()
    for chunk in range(fold):
        keep_copy(chunk).wait()
        for step in range(1, planes):
            x_copy(col, chunk, other_col(step)).wait_recv()

    zero = jnp.zeros((depth, size), jnp.bfloat16)
    block_cols = groups * fold

    def partial_tile(row_part, g):
        a = (plane * fold + row_part) * groups + g

        def step(slot_col, unused):
            lines = []
            for p in range(share):
                obs = obs_ref[a, slot_col * share + p]
                tiles = []
                for j in range(block_cols):
                    slot = place_ref[col * block_cols + j, obs]
                    safe = jnp.maximum(slot, 0)
                    tile = cols[safe // share, j // groups, j % groups, safe % share]
                    tiles.append(jnp.where(slot >= 0, tile, zero))
                lines.append(jnp.concatenate(tiles, axis=1))
            total[row_part, g] += jnp.dot(rows[slot_col, row_part, g], jnp.concatenate(lines, axis=0),
                                          preferred_element_type=jnp.float32)
            return unused

        total[row_part, g] = jnp.zeros(total.shape[2:], jnp.float32)
        lax.fori_loop(0, planes, step, 0)

    for step in range(1, fold):
        for g in range(groups):
            partial_tile(other_part(step), g)
            t_copy(step, g).start()
    for g in range(groups):
        partial_tile(part, g)

    for g in range(groups):
        update = total[part, g]
        for step in range(1, fold):
            t_copy(step, g).wait_recv()
            update = update + inbox[step - 1, g]
        across = pl.ds(g * size, size)
        for j in range(block_cols):
            a, b = row * groups + g, col * block_cols + j
            kept = pattern_ref[jnp.minimum(a, b), jnp.maximum(a, b)] == 1
            down = slice(j * size, (j + 1) * size)
            out_ref[across, down] = prior_ref[across, down] + jnp.where(
                kept, update[:, down], jnp.zeros((size, size), jnp.float32))

    for step in range(1, fold):
        y_copy(step, part).wait_send()
        for g in range(groups):
            t_copy(step, g).wait_send()
    for index in range(planes // 2):
        near_copy(col, index, col).wait_send()
    for step in far_steps:
        far_copy(step, col).wait_send()
    for chunk in range(fold):
        for step in range(1, planes):
            x_copy(other_col(step), chunk, col).wait_send()
        for from_plane in range(planes):
            @pl.when((from_plane <= plane) & (plane < planes - 1))
            def _():
                z_copy(0, from_plane, chunk).wait_send()

            @pl.when((from_plane >= plane) & (plane > 0))
            def _():
                z_copy(1, from_plane, chunk).wait_send()


def on_device(panels, obs_of, counts, inv_var, pattern, prior):
    planes = lax.axis_size("col")
    fold = lax.axis_size("row") // planes
    groups, share, size, _ = panels.shape
    depth = size // fold
    slots = jnp.arange(obs_of.shape[1], dtype=jnp.int32)
    ids = jnp.arange(inv_var.shape[0], dtype=jnp.int32)
    found = obs_of[:, None, :] == ids[None, :, None]
    place = jnp.max(jnp.where(found, slots[None, None, :], -1), axis=2)
    smem = pl.BlockSpec(memory_space=pltpu.SMEM)
    vmem = pl.BlockSpec(memory_space=pltpu.VMEM)
    dma = pltpu.SemaphoreType.DMA
    others = max(fold - 1, 1)
    panel = (fold, groups, share, depth, size)
    turned = (fold, groups, size, share * depth)
    tile = (groups, size, prior.shape[1])
    return pl.pallas_call(
        functools.partial(kernel, planes, fold),
        out_shape=jax.ShapeDtypeStruct(prior.shape, prior.dtype),
        in_specs=[smem, smem, smem, smem, vmem, vmem, vmem],
        out_specs=vmem,
        scratch_shapes=[
            pltpu.VMEM((size, groups * share), jnp.float32),
            pltpu.VMEM((others,) + panel[1:], jnp.bfloat16),
            pltpu.VMEM((planes,) + panel, jnp.bfloat16),
            pltpu.VMEM(turned, jnp.bfloat16),
            pltpu.VMEM((planes,) + turned, jnp.bfloat16),
            pltpu.VMEM((planes,) + panel, jnp.bfloat16),
            pltpu.VMEM((fold,) + tile, jnp.float32),
            pltpu.VMEM((others,) + tile, jnp.float32),
            dma((others,)), dma((fold,)),
            dma((2, planes, fold)), dma((planes, fold)),
            dma((planes, fold)), dma((planes, fold)),
            dma((planes,)), dma((planes,)),
            dma((planes // 2,)), dma((planes // 2,)),
            dma((others, groups)), dma((others, groups)),
            dma((fold + 1,)),
        ],
        compiler_params=pltpu.CompilerParams(
            collective_id=0, has_side_effects=True, vmem_limit_bytes=48 * 1024 * 1024),
    )(obs_of, counts, place, pattern, inv_var, panels, prior)


def solution(mesh):
    placed = (P("row", "col", None, None), P(), P(), P(), P(), P("row", "col"))
    return jax.shard_map(
        on_device, mesh=mesh, in_specs=placed, out_specs=P("row", "col"), check_vma=False
    )
```

time: 232 us -> 63.2 us (0.27)
  the two profiles are of different devices: /device:TPU:24 before, /device:TPU:0 now
where the time goes in v2:
time: 63.2 us; the launch traced here: 62.9 us
  Pallas kernels  57.6 us (91%)
  local copies, waits for them, and re-layouts  4.29 us (7%)
  other arithmetic  0.92 us (1%)
    pallas_call x1, Pallas kernels, on_device(): pl.pallas_call(functools.partial(kernel, planes, fold), out_shape=jax.Sha...  57.6 us
    unnamed x13, local copies, waits for them, and re-layouts  4.29 us

profile of v2, /device:TPU:0, one launch (start us, length us, event | category | flops | bytes accessed | tf_op | source)
XLA Modules:
  0.0 62.9 jit_solution(180953090314323875)
XLA Ops:
  0.0 0.0 copy-start.2
  0.0 0.0 copy-start.4
  0.0 0.9 %select_reduce_fusion.place_ref = s32[16,64]{1,0:T(8,128)S(1)} fusion(s32[16,32]{1,0:T(8,128)} %obs_ref.1), kind=kLoop, calls=%fused_computation | loop fusion | flops 97280 | bytes 6144 | tf_op jit(solution)/shard_map/reduce_max | solution.py:253
  0.9 0.0 copy-done.2
  0.9 0.0 copy-done.4
  1.0 0.0 copy-start
  1.0 1.0 %copy-done = bf16[2,8,128,128]{3,2,1,0:T(8,128)(2,1)S(1)} copy-done((bf16[2,8,128,128]{3,2,1,0:T(8,128)(2,1)S(1)}, bf16[2,8,128,128]{3,2,1,0:T(8,128)(2,1)}, u32[]{:S(2)}) %copy-start) | copy-done | bytes 524312
  2.0 0.0 copy-start.1
  2.0 1.0 %copy-done.1 = f32[256,512]{1,0:T(8,128)S(1)} copy-done((f32[256,512]{1,0:T(8,128)S(1)}, f32[256,512]{1,0:T(8,128)}, u32[]{:S(2)}) %copy-start.1) | copy-done | bytes 524312
  3.0 0.0 copy-start.3
  3.0 0.8 %copy-done.3 = f32[64,128]{1,0:T(8,128)S(1)} copy-done((f32[64,128]{1,0:T(8,128)S(1)}, f32[64,128]{1,0:T(8,128)}, u32[]{:S(2)}) %copy-start.3) | copy-done | bytes 32792
  3.8 0.0 copy-start.5
  3.8 0.7 %copy-done.5 = s32[16]{0:T(128)S(1)} copy-done((s32[16]{0:T(128)S(1)}, s32[16]{0:T(128)}, u32[]{:S(2)}) %copy-start.5) | copy-done | bytes 88
  4.5 57.6 %shard_map.64 = f32[256,512]{1,0:T(8,128)S(1)} custom-call(s32[16,32]{1,0:T(8,128)S(1)} %copy-done.2, s32[16]{0:T(128)S(1)} %copy-done.5, s32[16,64]{1,0:T(8,128)S(1)} %select_reduce_fusion.place_ref, s32[16,16]{1,0:T(8,128)S(1)} %copy-done.4, f32[64,128]{1,0:T(8,128)S(1)} %copy-done.3, bf16[2,8,128,128]{3,2,1,0:T(8,128)(2,1)S(1)} %copy-done, ...), custom_call_target="tpu_custom_call" | custom-call | tf_op jit(solution)/shard_map/pallas_call | solution.py:261
  62.1 0.8 %copy.8 = f32[256,512]{1,0:T(8,128)} copy(f32[256,512]{1,0:T(8,128)S(1)} %shard_map.64) | data formatting | bytes 1048576
Async XLA Ops:
  0.0 0.9 %copy-start.2 = (s32[16,32]{1,0:T(8,128)S(1)}, s32[16,32]{1,0:T(8,128)}, u32[]{:S(2)}) copy-start(s32[16,32]{1,0:T(8,128)} %obs_ref.1) | copy-start | bytes 6148
  0.0 0.9 %copy-start.4 = (s32[16,16]{1,0:T(8,128)S(1)}, s32[16,16]{1,0:T(8,128)}, u32[]{:S(2)}) copy-start(s32[16,16]{1,0:T(8,128)} %pattern_ref.1) | copy-start | bytes 3076
  1.0 1.0 %copy-start = (bf16[2,8,128,128]{3,2,1,0:T(8,128)(2,1)S(1)}, bf16[2,8,128,128]{3,2,1,0:T(8,128)(2,1)}, u32[]{:S(2)}) copy-start(bf16[2,8,128,128]{3,2,1,0:T(8,128)(2,1)} %panels_ref.1) | copy-start | bytes 1572868
  2.0 1.0 %copy-start.1 = (f32[256,512]{1,0:T(8,128)S(1)}, f32[256,512]{1,0:T(8,128)}, u32[]{:S(2)}) copy-start(f32[256,512]{1,0:T(8,128)} %prior_ref.1) | copy-start | bytes 1572868
  3.0 0.8 %copy-start.3 = (f32[64,128]{1,0:T(8,128)S(1)}, f32[64,128]{1,0:T(8,128)}, u32[]{:S(2)}) copy-start(f32[64,128]{1,0:T(8,128)} %var_ref.1) | copy-start | bytes 98308
  3.8 0.7 %copy-start.5 = (s32[16]{0:T(128)S(1)}, s32[16]{0:T(128)}, u32[]{:S(2)}) copy-start(s32[16]{0:T(128)} %counts_ref.1) | copy-start | bytes 196

commit v3 on v2

v3 whole, which is shorter than its diff:
```python
import functools

import jax
import jax.numpy as jnp
from jax import lax
from jax.experimental import pallas as pl
from jax.experimental.pallas import tpu as pltpu
from jax.sharding import PartitionSpec as P

MESH = pl.DeviceIdType.MESH


def kernel(planes, fold, obs_ref, counts_ref, place_ref, pattern_ref, var_ref, source_ref, out_ref,
           panels_ref, weights, leaving, held, turned, rows, cols, total, inbox,
           y_send, y_recv, z_send, z_recv, x_send, x_recv, r_send, r_recv, n_send, n_recv,
           t_send, t_recv, keep, fetch):
    row, col = lax.axis_index("row"), lax.axis_index("col")
    plane, part = row // fold, row % fold
    groups, share, size = panels_ref.shape[0], panels_ref.shape[1], panels_ref.shape[2]
    depth = size // fold
    wide = share * depth
    near = col + 1 - 2 * lax.rem(col, 2)
    far_steps = range(2, planes, 2)

    def at(other_row, other_col):
        return {"row": other_row, "col": other_col}

    def other_plane(step):
        return lax.rem(plane + step, planes)

    def other_col(step):
        return lax.rem(col + step, planes)

    def other_part(step):
        return lax.rem(part + step, fold)

    fetched = pltpu.make_async_copy(source_ref, panels_ref, fetch)
    fetched.start()
    partners = [at(other_plane(s) * fold + part, col) for s in (1, planes - 1)]
    partners += [at(row, other_col(s)) for s in range(1, planes)]
    partners += [at(plane * fold + other_part(s), col) for s in range(1, fold)]
    barrier = pltpu.get_barrier_semaphore()
    for partner in partners:
        pl.semaphore_signal(barrier, inc=1, device_id=partner, device_id_type=MESH)

    factors = []
    for g in range(groups):
        block = row * groups + g
        for p in range(share):
            slot = col * share + p
            live = jnp.where(slot < counts_ref[block], 1.0, 0.0)
            factors.append(jnp.sqrt(var_ref[pl.ds(obs_ref[block, slot], 1), :]) * live)
    weights[...] = jnp.concatenate(factors, axis=0).T
    fetched.wait()

    def scaled(to_part, g, p):
        j = g * share + p
        lines = pl.ds(pl.multiple_of(to_part * depth, depth), depth)
        value = panels_ref[g, p, lines, :].astype(jnp.float32) * weights[lines, j:j + 1]
        return value.astype(jnp.bfloat16)

    def copy(src, dst, send, recv, device):
        return pltpu.make_async_remote_copy(
            src_ref=src, dst_ref=dst, send_sem=send, recv_sem=recv,
            device_id=device, device_id_type=MESH)

    def y_copy(step, g, landing):
        return copy(leaving.at[step - 1, g], held.at[plane, landing, g], y_send.at[step - 1, g],
                    y_recv.at[landing, g], at(plane * fold + other_part(step), col))

    def z_copy(way, from_plane, chunk, g):
        target = lax.rem(plane + (1 if way == 0 else planes - 1), planes)
        return copy(held.at[from_plane, chunk, g], held.at[from_plane, chunk, g],
                    z_send.at[way, from_plane, chunk, g], z_recv.at[from_plane, chunk, g],
                    at(target * fold + part, col))

    def x_copy(to_col, order, g, landing):
        return copy(held.at[to_col, other_part(order), g], cols[order].at[landing, g],
                    x_send.at[to_col, order, g], x_recv.at[landing, order, g], at(row, to_col))

    def keep_copy(order, g):
        return pltpu.make_async_copy(held.at[col, other_part(order), g], cols[order].at[col, g],
                                     keep.at[order, g])

    def far_copy(step, landing):
        return copy(turned, rows.at[landing], r_send.at[step], r_recv.at[landing], at(row, other_col(step)))

    def near_copy(slot, index, landing):
        source = turned if index == 0 else rows.at[slot]
        return copy(source, rows.at[landing], n_send.at[index], n_recv.at[index], at(row, near))

    def t_copy(step, chunk, g):
        return copy(total.at[other_part(step), chunk, g], inbox.at[step - 1, chunk, g],
                    t_send.at[step - 1, chunk, g], t_recv.at[step - 1, chunk, g],
                    at(plane * fold + other_part(step), col))

    def spread(from_plane, order, g):
        @pl.when(from_plane != col)
        def _():
            x_copy(from_plane, order, g, col).start()

        @pl.when(from_plane == col)
        def _():
            keep_copy(order, g).start()

    def begin(chunk, g):
        @pl.when(plane < planes - 1)
        def _():
            z_copy(0, plane, chunk, g).start()

        @pl.when(plane > 0)
        def _():
            z_copy(1, plane, chunk, g).start()

    def turn(chunk, g):
        turned[chunk, g] = held[plane, chunk, g].reshape(wide, size).T

    for step in range(1, fold):
        for g in range(groups):
            for p in range(share):
                leaving[step - 1, g, p] = scaled(other_part(step), g, p)
    pl.semaphore_wait(barrier, len(partners))
    for step in range(1, fold):
        for g in range(groups):
            y_copy(step, g, part).start()
    for g in range(groups):
        for p in range(share):
            held[plane, part, g, p] = scaled(part, g, p)
        begin(part, g)
    for g in range(groups):
        spread(plane, 0, g)
        turn(part, g)
    for step in range(1, fold):
        for g in range(groups):
            y_copy(step, g, other_part(step)).wait_recv()
            begin(other_part(step), g)
        for g in range(groups):
            spread(plane, step, g)
            turn(other_part(step), g)
    own_row = pltpu.make_async_copy(turned, rows.at[col], fetch)
    own_row.start()
    near_copy(col, 0, col).start()
    for step in far_steps:
        far_copy(step, col).start()

    def pass_rows():
        for index, step in enumerate(far_steps):
            slot = other_col(step)
            far_copy(step, slot).wait_recv()
            near_copy(slot, index + 1, slot).start()

    for step in range(1, planes):
        below, above = plane - step, plane + step
        for order in range(fold):
            chunk = other_part(order)
            for g in range(groups):
                @pl.when(below >= 0)
                def _():
                    z_copy(0, below, chunk, g).wait_recv()

                    @pl.when(plane < planes - 1)
                    def _():
                        z_copy(0, below, chunk, g).start()

                    spread(below, order, g)

                @pl.when(above < planes)
                def _():
                    z_copy(1, above, chunk, g).wait_recv()

                    @pl.when(plane > 0)
                    def _():
                        z_copy(1, above, chunk, g).start()

                    spread(above, order, g)
        if step == min(2, planes - 1):
            pass_rows()

    own_row.wait()
    near_copy(near, 0, near).wait_recv()
    for index, step in enumerate(far_steps):
        slot = lax.rem(near + step, planes)
        near_copy(slot, index + 1, slot).wait_recv()
    zero = jnp.zeros((depth, size), jnp.bfloat16)
    block_cols = groups * fold

    def partial_tiles(row_part, order):
        chunk = other_part(order)

        def step(slot_col, unused):
            for g in range(groups):
                a = (plane * fold + row_part) * groups + g
                lines = []
                for p in range(share):
                    obs = obs_ref[a, slot_col * share + p]
                    tiles = []
                    for h in range(groups):
                        slot = place_ref[col * block_cols + chunk * groups + h, obs]
                        safe = jnp.maximum(slot, 0)
                        tile = cols[order][safe // share, h, safe % share]
                        tiles.append(jnp.where(slot >= 0, tile, zero))
                    lines.append(jnp.concatenate(tiles, axis=1))
                total[row_part, chunk, g] += jnp.dot(
                    rows[slot_col, row_part, g], jnp.concatenate(lines, axis=0),
                    preferred_element_type=jnp.float32)
            return unused

        total[row_part, chunk] = jnp.zeros(total.shape[2:], jnp.float32)
        lax.fori_loop(0, planes, step, 0)

    for order in range(fold):
        chunk = other_part(order)
        for g in range(groups):
            keep_copy(order, g).wait()
            for step in range(1, planes):
                x_copy(col, order, g, other_col(step)).wait_recv()
        for step in range(1, fold):
            partial_tiles(other_part(step), order)
            for g in range(groups):
                t_copy(step, chunk, g).start()
        partial_tiles(part, order)

    for order in range(fold):
        chunk = other_part(order)
        for g in range(groups):
            update = total[part, chunk, g]
            for step in range(1, fold):
                t_copy(step, chunk, g).wait_recv()
                update = update + inbox[step - 1, chunk, g]
            for h in range(groups):
                a, b = row * groups + g, col * block_cols + chunk * groups + h
                kept = pattern_ref[jnp.minimum(a, b), jnp.maximum(a, b)] == 1
                down = pl.ds(pl.multiple_of((chunk * groups + h) * size, size), size)
                out_ref[g * size:(g + 1) * size, down] = jnp.where(
                    kept, update[:, h * size:(h + 1) * size], jnp.zeros((size, size), jnp.float32))

    for step in range(1, fold):
        for g in range(groups):
            y_copy(step, g, part).wait_send()
            for chunk in range(fold):
                t_copy(step, chunk, g).wait_send()
    for index in range(planes // 2):
        near_copy(col, index, col).wait_send()
    for step in far_steps:
        far_copy(step, col).wait_send()
    for chunk in range(fold):
        for g in range(groups):
            for step in range(1, planes):
                x_copy(other_col(step), chunk, g, col).wait_send()
            for from_plane in range(planes):
                @pl.when((from_plane <= plane) & (plane < planes - 1))
                def _():
                    z_copy(0, from_plane, chunk, g).wait_send()

                @pl.when((from_plane >= plane) & (plane > 0))
                def _():
                    z_copy(1, from_plane, chunk, g).wait_send()


def on_device(panels, obs_of, counts, inv_var, pattern, prior):
    planes = lax.axis_size("col")
    fold = lax.axis_size("row") // planes
    groups, share, size, _ = panels.shape
    depth = size // fold
    slots = jnp.arange(obs_of.shape[1], dtype=jnp.int32)
    ids = jnp.arange(inv_var.shape[0], dtype=jnp.int32)
    found = obs_of[:, None, :] == ids[None, :, None]
    place = jnp.max(jnp.where(found, slots[None, None, :], -1), axis=2)
    smem = pl.BlockSpec(memory_space=pltpu.SMEM)
    vmem = pl.BlockSpec(memory_space=pltpu.VMEM)
    dma = pltpu.SemaphoreType.DMA
    others = max(fold - 1, 1)
    panel = (fold, groups, share, depth, size)
    turned = (fold, groups, size, share * depth)
    tile = (fold, groups, size, groups * size)
    update = pl.pallas_call(
        functools.partial(kernel, planes, fold),
        out_shape=jax.ShapeDtypeStruct(prior.shape, prior.dtype),
        in_specs=[smem, smem, smem, smem, vmem, pl.BlockSpec(memory_space=pl.ANY)],
        out_specs=vmem,
        scratch_shapes=[
            pltpu.VMEM(panels.shape, jnp.bfloat16),
            pltpu.VMEM((size, groups * share), jnp.float32),
            pltpu.VMEM((others,) + panel[1:], jnp.bfloat16),
            pltpu.VMEM((planes,) + panel, jnp.bfloat16),
            pltpu.VMEM(turned, jnp.bfloat16),
            pltpu.VMEM((planes,) + turned, jnp.bfloat16),
            (pltpu.VMEM((planes,) + panel[1:], jnp.bfloat16),) * fold,
            pltpu.VMEM((fold,) + tile, jnp.float32),
            pltpu.VMEM((others,) + tile, jnp.float32),
            dma((others, groups)), dma((fold, groups)),
            dma((2, planes, fold, groups)), dma((planes, fold, groups)),
            dma((planes, fold, groups)), dma((planes, fold, groups)),
            dma((planes,)), dma((planes,)),
            dma((planes // 2,)), dma((planes // 2,)),
            dma((others, fold, groups)), dma((others, fold, groups)),
            dma((fold, groups)), dma,
        ],
        compiler_params=pltpu.CompilerParams(
            collective_id=0, has_side_effects=True, vmem_limit_bytes=60 * 1024 * 1024),
    )(obs_of, counts, place, pattern, inv_var, panels)
    return prior + update


def solution(mesh):
    placed = (P("row", "col", None, None), P(), P(), P(), P(), P("row", "col"))
    return jax.shard_map(
        on_device, mesh=mesh, in_specs=placed, out_specs=P("row", "col"), check_vma=False
    )
```

time: 63.2 us -> 61 us (0.965)
  local copies, waits for them, and re-layouts: 4.29 us -> 0.01 us
  other arithmetic: 0.92 us -> 3.37 us
    unnamed x13 -> x2, local copies, waits for them, and re-layouts: 4.29 us -> 0.01 us
    add x0 -> x1, other arithmetic: none -> 1.91 us  [on_device(): return prior + update]
where the time goes in v3:
time: 61 us; the launch traced here: 60.7 us
  Pallas kernels  57.4 us (94%)
  other arithmetic  3.37 us (6%)
    pallas_call x1, Pallas kernels, on_device(): pl.pallas_call(functools.partial(kernel, planes, fold), out_shape=jax.Sha...  57.4 us
    add x1, other arithmetic, on_device(): return prior + update  1.91 us
    reduce_max x1, other arithmetic, on_device(): place = jnp.max(jnp.where(found, slots[None, None, :], -1), axis=2)  1.45 us

profile of v3, /device:TPU:0, one launch (start us, length us, event | category | flops | bytes accessed | tf_op | source)
XLA Modules:
  0.0 60.7 jit_solution(13451451011795746193)
XLA Ops:
  0.0 1.5 %select_reduce_fusion.place_ref = s32[16,64]{1,0:T(8,128)} fusion(s32[16,32]{1,0:T(8,128)} %obs_ref.1), kind=kLoop, calls=%fused_computation | loop fusion | flops 97280 | bytes 6144 | tf_op jit(solution)/shard_map/reduce_max | solution.py:268
  1.5 0.0 copy-start
  1.5 57.4 %shard_map.64 = f32[256,512]{1,0:T(8,128)} custom-call(s32[16,32]{1,0:T(8,128)} %obs_ref.1, s32[16]{0:T(128)} %counts_ref.1, s32[16,64]{1,0:T(8,128)} %select_reduce_fusion.place_ref, s32[16,16]{1,0:T(8,128)} %pattern_ref.1, f32[64,128]{1,0:T(8,128)} %var_ref.1, bf16[2,8,128,128]{3,2,1,0:T(8,128)(2,1)} %source_ref.1), custom_call_target="tpu_custom_call" | custom-call | tf_op jit(solution)/shard_map/pallas_call | solution.py:276
  58.8 0.0 copy-done
  58.8 1.9 %add.3 = f32[256,512]{1,0:T(8,128)} add(f32[256,512]{1,0:T(8,128)S(1)} %copy-done, f32[256,512]{1,0:T(8,128)} %shard_map.64) | non-fusion elementwise | flops 131072 | bytes 1572864 | tf_op jit(solution)/shard_map/add | solution.py:302
Async XLA Ops:
  1.5 57.4 %copy-start = (f32[256,512]{1,0:T(8,128)S(1)}, f32[256,512]{1,0:T(8,128)}, u32[]{:S(2)}) copy-start(f32[256,512]{1,0:T(8,128)} %param.11) | copy-start | bytes 1572868

commit v4 on v3

--- a/solution.py
+++ b/solution.py
@@ -10,10 +10,10 @@
 MESH = pl.DeviceIdType.MESH
 
 
-def kernel(planes, fold, obs_ref, counts_ref, place_ref, pattern_ref, var_ref, source_ref, out_ref,
-           panels_ref, weights, leaving, held, turned, rows, cols, total, inbox,
+def kernel(planes, fold, obs_ref, counts_ref, pattern_ref, ids_ref, var_ref, source_ref, prior_source, out_ref,
+           panels_ref, prior_ref, table, place_ref, weights, leaving, held, turned, rows, cols, total, inbox,
            y_send, y_recv, z_send, z_recv, x_send, x_recv, r_send, r_recv, n_send, n_recv,
-           t_send, t_recv, keep, fetch):
+           t_send, t_recv, keep, fetch, prior_fetch, place_fetch):
     row, col = lax.axis_index("row"), lax.axis_index("col")
     plane, part = row // fold, row % fold
     groups, share, size = panels_ref.shape[0], panels_ref.shape[1], panels_ref.shape[2]
@@ -36,6 +36,8 @@
 
     fetched = pltpu.make_async_copy(source_ref, panels_ref, fetch)
     fetched.start()
+    prior_fetched = pltpu.make_async_copy(prior_source, prior_ref, prior_fetch)
+    prior_fetched.start()
     partners = [at(other_plane(s) * fold + part, col) for s in (1, planes - 1)]
     partners += [at(row, other_col(s)) for s in range(1, planes)]
     partners += [at(plane * fold + other_part(s), col) for s in range(1, fold)]
@@ -137,6 +139,13 @@
         for g in range(groups):
             spread(plane, step, g)
             turn(other_part(step), g)
+    ids = lax.broadcasted_iota(jnp.int32, table.shape, 1)
+    found = jnp.full(table.shape, -1, jnp.int32)
+    for p in range(ids_ref.shape[1]):
+        found = jnp.where(ids_ref[:, p:p + 1] == ids, p, found)
+    table[...] = found
+    placed = pltpu.make_async_copy(table, place_ref, place_fetch)
+    placed.start()
     own_row = pltpu.make_async_copy(turned, rows.at[col], fetch)
     own_row.start()
     near_copy(col, 0, col).start()
@@ -149,43 +158,11 @@
             far_copy(step, slot).wait_recv()
             near_copy(slot, index + 1, slot).start()
 
-    for step in range(1, planes):
-        below, above = plane - step, plane + step
-        for order in range(fold):
-            chunk = other_part(order)
-            for g in range(groups):
-                @pl.when(below >= 0)
-                def _():
-                    z_copy(0, below, chunk, g).wait_recv()
-
-                    @pl.when(plane < planes - 1)
-                    def _():
-                        z_copy(0, below, chunk, g).start()
-
-                    spread(below, order, g)
-
-                @pl.when(above < planes)
-                def _():
-                    z_copy(1, above, chunk, g).wait_recv()
-
-                    @pl.when(plane > 0)
-                    def _():
-                        z_copy(1, above, chunk, g).start()
-
-                    spread(above, order, g)
-        if step == min(2, planes - 1):
-            pass_rows()
-
-    own_row.wait()
-    near_copy(near, 0, near).wait_recv()
-    for index, step in enumerate(far_steps):
-        slot = lax.rem(near + step, planes)
-        near_copy(slot, index + 1, slot).wait_recv()
     zero = jnp.zeros((depth, size), jnp.bfloat16)
     block_cols = groups * fold
 
-    def partial_tiles(row_part, order):
-        chunk = other_part(order)
+    def partial_tiles(step_part, order):
+        row_part, chunk = other_part(step_part), other_part(order)
 
         def step(slot_col, unused):
             for g in range(groups):
@@ -207,19 +184,83 @@
 
         total[row_part, chunk] = jnp.zeros(total.shape[2:], jnp.float32)
         lax.fori_loop(0, planes, step, 0)
-
-    for order in range(fold):
-        chunk = other_part(order)
+        if step_part > 0:
+            for g in range(groups):
+                t_copy(step_part, chunk, g).start()
+
+    def await_rows():
+        placed.wait()
+        own_row.wait()
+        near_copy(near, 0, near).wait_recv()
+        for index, step in enumerate(far_steps):
+            slot = lax.rem(near + step, planes)
+            near_copy(slot, index + 1, slot).wait_recv()
+
+    def await_columns(order):
         for g in range(groups):
             keep_copy(order, g).wait()
             for step in range(1, planes):
                 x_copy(col, order, g, other_col(step)).wait_recv()
-        for step in range(1, fold):
-            partial_tiles(other_part(step), order)
+
+    distance = jnp.maximum(plane - col, col - plane)
+    units = [(step, order) for step in range(1, fold) for order in range(fold)]
+    units += [(0, order) for order in range(fold)]
+
+    def products_between(piece):
+        pieces = fold * groups
+        mine = units[piece * len(units) // pieces:(piece + 1) * len(units) // pieces]
+        if not mine:
+            return
+
+        @pl.when(distance < planes - 1)
+        def _():
+            if mine[0] == units[0]:
+                await_rows()
+            for unit in mine:
+                if unit in units[:fold]:
+                    await_columns(unit[1])
+                partial_tiles(*unit)
+
+    for step in range(1, planes):
+        below, above = plane - step, plane + step
+        for order in range(fold):
+            chunk = other_part(order)
             for g in range(groups):
-                t_copy(step, chunk, g).start()
-        partial_tiles(part, order)
-
+                @pl.when(below >= 0)
+                def _():
+                    z_copy(0, below, chunk, g).wait_recv()
+
+                    @pl.when(plane < planes - 1)
+                    def _():
+                        z_copy(0, below, chunk, g).start()
+
+                    spread(below, order, g)
+
+                @pl.when(above < planes)
+                def _():
+                    z_copy(1, above, chunk, g).wait_recv()
+
+                    @pl.when(plane > 0)
+                    def _():
+                        z_copy(1, above, chunk, g).start()
+
+                    spread(above, order, g)
+
+                if step == planes - 1:
+                    products_between(order * groups + g)
+                elif step == planes - 2 and order * groups + g == min(1, fold * groups - 1):
+                    pass_rows()
+
+    @pl.when(distance == planes - 1)
+    def _():
+        await_rows()
+        for order in range(fold):
+            await_columns(order)
+            for step in range(1, fold):
+                partial_tiles(step, order)
+            partial_tiles(0, order)
+
+    prior_fetched.wait()
     for order in range(fold):
         chunk = other_part(order)
         for g in range(groups):
@@ -231,7 +272,8 @@
                 a, b = row * groups + g, col * block_cols + chunk * groups + h
                 kept = pattern_ref[jnp.minimum(a, b), jnp.maximum(a, b)] == 1
                 down = pl.ds(pl.multiple_of((chunk * groups + h) * size, size), size)
-                out_ref[g * size:(g + 1) * size, down] = jnp.where(
+                across = slice(g * size, (g + 1) * size)
+                out_ref[across, down] = prior_ref[across, down] + jnp.where(
                     kept, update[:, h * size:(h + 1) * size], jnp.zeros((size, size), jnp.float32))
 
     for step in range(1, fold):
@@ -262,24 +304,25 @@
     fold = lax.axis_size("row") // planes
     groups, share, size, _ = panels.shape
     depth = size // fold
-    slots = jnp.arange(obs_of.shape[1], dtype=jnp.int32)
-    ids = jnp.arange(inv_var.shape[0], dtype=jnp.int32)
-    found = obs_of[:, None, :] == ids[None, :, None]
-    place = jnp.max(jnp.where(found, slots[None, None, :], -1), axis=2)
+    names = -(-inv_var.shape[0] // 128) * 128
     smem = pl.BlockSpec(memory_space=pltpu.SMEM)
     vmem = pl.BlockSpec(memory_space=pltpu.VMEM)
+    anywhere = pl.BlockSpec(memory_space=pl.ANY)
     dma = pltpu.SemaphoreType.DMA
     others = max(fold - 1, 1)
     panel = (fold, groups, share, depth, size)
     turned = (fold, groups, size, share * depth)
     tile = (fold, groups, size, groups * size)
-    update = pl.pallas_call(
+    return pl.pallas_call(
         functools.partial(kernel, planes, fold),
         out_shape=jax.ShapeDtypeStruct(prior.shape, prior.dtype),
-        in_specs=[smem, smem, smem, smem, vmem, pl.BlockSpec(memory_space=pl.ANY)],
+        in_specs=[smem, smem, smem, vmem, vmem, anywhere, anywhere],
         out_specs=vmem,
         scratch_shapes=[
             pltpu.VMEM(panels.shape, jnp.bfloat16),
+            pltpu.VMEM(prior.shape, jnp.float32),
+            pltpu.VMEM((obs_of.shape[0], names), jnp.int32),
+            pltpu.SMEM((obs_of.shape[0], names), jnp.int32),
             pltpu.VMEM((size, groups * share), jnp.float32),
             pltpu.VMEM((others,) + panel[1:], jnp.bfloat16),
             pltpu.VMEM((planes,) + panel, jnp.bfloat16),
@@ -294,12 +337,11 @@
             dma((planes,)), dma((planes,)),
             dma((planes // 2,)), dma((planes // 2,)),
             dma((others, fold, groups)), dma((others, fold, groups)),
-            dma((fold, groups)), dma,
+            dma((fold, groups)), dma, dma, dma,
         ],
         compiler_params=pltpu.CompilerParams(
             collective_id=0, has_side_effects=True, vmem_limit_bytes=60 * 1024 * 1024),
-    )(obs_of, counts, place, pattern, inv_var, panels)
-    return prior + update
+    )(obs_of, counts, pattern, obs_of, inv_var, panels, prior)
 
 
 def solution(mesh):

time: 61 us -> 58 us (0.951)
  the two profiles are of different devices: /device:TPU:0 before, /device:TPU:24 now
where the time goes in v4:
time: 58 us; the launch traced here: 57.7 us
  Pallas kernels  55.9 us (96%)
  local copies, waits for them, and re-layouts  1.87 us (3%)
    pallas_call x1, Pallas kernels, on_device(): pl.pallas_call(functools.partial(kernel, planes, fold), out_shape=jax.Sha...  55.9 us
    unnamed x1, local copies, waits for them, and re-layouts  1.87 us

profile of v4, /device:TPU:24, one launch (start us, length us, event | category | flops | bytes accessed | tf_op | source)
XLA Modules:
  0.0 57.7 jit_solution(1037638665443150164)
XLA Ops:
  0.0 55.9 %shard_map.64 = f32[256,512]{1,0:T(8,128)} custom-call(s32[16,32]{1,0:T(8,128)} %ids_ref.1, s32[16]{0:T(128)} %counts_ref.1, s32[16,16]{1,0:T(8,128)} %pattern_ref.1, s32[16,32]{1,0:T(8,128)} %ids_ref.1, f32[64,128]{1,0:T(8,128)} %var_ref.1, bf16[2,8,128,128]{3,2,1,0:T(8,128)(2,1)} %source_ref.1, f32[256,512]{1,0:T(8,128)} %prior_source.1), custom_call_target="tpu_custom_call" | custom-call | tf_op jit(solution)/shard_map/pallas_call | solution.py:316
  55.9 1.9 %copy.8 = f32[256,512]{1,0:T(8,128)} copy(f32[256,512]{1,0:T(8,128)} %shard_map.64) | data formatting | bytes 1048576

commit v5 on v4

--- a/solution.py
+++ b/solution.py
@@ -19,6 +19,7 @@
     groups, share, size = panels_ref.shape[0], panels_ref.shape[1], panels_ref.shape[2]
     depth = size // fold
     wide = share * depth
+    slot_count = ids_ref.shape[1]
     near = col + 1 - 2 * lax.rem(col, 2)
     far_steps = range(2, planes, 2)
 
@@ -76,12 +77,15 @@
                     z_send.at[way, from_plane, chunk, g], z_recv.at[from_plane, chunk, g],
                     at(target * fold + part, col))
 
+    def slots_of(slot_col):
+        return pl.ds(slot_col * share, share)
+
     def x_copy(to_col, order, g, landing):
-        return copy(held.at[to_col, other_part(order), g], cols[order].at[landing, g],
+        return copy(held.at[to_col, other_part(order), g], cols[order].at[g, slots_of(landing)],
                     x_send.at[to_col, order, g], x_recv.at[landing, order, g], at(row, to_col))
 
     def keep_copy(order, g):
-        return pltpu.make_async_copy(held.at[col, other_part(order), g], cols[order].at[col, g],
+        return pltpu.make_async_copy(held.at[col, other_part(order), g], cols[order].at[g, slots_of(col)],
                                      keep.at[order, g])
 
     def far_copy(step, landing):
@@ -140,12 +144,15 @@
             spread(plane, step, g)
             turn(other_part(step), g)
     ids = lax.broadcasted_iota(jnp.int32, table.shape, 1)
-    found = jnp.full(table.shape, -1, jnp.int32)
-    for p in range(ids_ref.shape[1]):
+    found = jnp.full(table.shape, slot_count, jnp.int32)
+    for p in range(slot_count):
         found = jnp.where(ids_ref[:, p:p + 1] == ids, p, found)
     table[...] = found
     placed = pltpu.make_async_copy(table, place_ref, place_fetch)
     placed.start()
+    for order in range(fold):
+        for h in range(groups):
+            cols[order][h, slot_count] = jnp.zeros((depth, size), jnp.bfloat16)
     own_row = pltpu.make_async_copy(turned, rows.at[col], fetch)
     own_row.start()
     near_copy(col, 0, col).start()
@@ -158,34 +165,30 @@
             far_copy(step, slot).wait_recv()
             near_copy(slot, index + 1, slot).start()
 
-    zero = jnp.zeros((depth, size), jnp.bfloat16)
     block_cols = groups * fold
+    paired = 2 if planes % 2 == 0 else 1
 
     def partial_tiles(step_part, order):
         row_part, chunk = other_part(step_part), other_part(order)
-
-        def step(slot_col, unused):
-            for g in range(groups):
-                a = (plane * fold + row_part) * groups + g
-                lines = []
-                for p in range(share):
-                    obs = obs_ref[a, slot_col * share + p]
-                    tiles = []
-                    for h in range(groups):
-                        slot = place_ref[col * block_cols + chunk * groups + h, obs]
-                        safe = jnp.maximum(slot, 0)
-                        tile = cols[order][safe // share, h, safe % share]
-                        tiles.append(jnp.where(slot >= 0, tile, zero))
-                    lines.append(jnp.concatenate(tiles, axis=1))
-                total[row_part, chunk, g] += jnp.dot(
-                    rows[slot_col, row_part, g], jnp.concatenate(lines, axis=0),
-                    preferred_element_type=jnp.float32)
-            return unused
-
-        total[row_part, chunk] = jnp.zeros(total.shape[2:], jnp.float32)
-        lax.fori_loop(0, planes, step, 0)
-        if step_part > 0:
-            for g in range(groups):
+        first = col * block_cols + chunk * groups
+        for g in range(groups):
+            a = (plane * fold + row_part) * groups + g
+
+            def step(i, unused):
+                for slot_col in [i * paired + k for k in range(paired)]:
+                    lines = []
+                    for p in range(share):
+                        obs = obs_ref[a, slot_col * share + p]
+                        lines.append(jnp.concatenate(
+                            [cols[order][h, place_ref[first + h, obs]] for h in range(groups)], axis=1))
+                    total[row_part, chunk, g] += jnp.dot(
+                        rows[slot_col, row_part, g], jnp.concatenate(lines, axis=0),
+                        preferred_element_type=jnp.float32)
+                return unused
+
+            total[row_part, chunk, g] = jnp.zeros(total.shape[3:], jnp.float32)
+            lax.fori_loop(0, planes // paired, step, 0)
+            if step_part > 0:
                 t_copy(step_part, chunk, g).start()
 
     def await_rows():
@@ -328,7 +331,7 @@
             pltpu.VMEM((planes,) + panel, jnp.bfloat16),
             pltpu.VMEM(turned, jnp.bfloat16),
             pltpu.VMEM((planes,) + turned, jnp.bfloat16),
-            (pltpu.VMEM((planes,) + panel[1:], jnp.bfloat16),) * fold,
+            (pltpu.VMEM((groups, obs_of.shape[1] + 1, depth, size), jnp.bfloat16),) * fold,
             pltpu.VMEM((fold,) + tile, jnp.float32),
             pltpu.VMEM((others,) + tile, jnp.float32),
             dma((others, groups)), dma((fold, groups)),

time: 58 us -> 56.3 us (0.971)
  Pallas kernels: 55.9 us -> 54 us
    pallas_call x1, Pallas kernels: 55.9 us -> 54 us  [on_device(): pl.pallas_call(functools.partial(kernel, planes, fold), out_shape=jax.Sha...]
where the time goes in v5:
time: 56.3 us; the launch traced here: 55.9 us
  Pallas kernels  54 us (96%)
  local copies, waits for them, and re-layouts  1.87 us (3%)
    pallas_call x1, Pallas kernels, on_device(): pl.pallas_call(functools.partial(kernel, planes, fold), out_shape=jax.Sha...  54 us
    unnamed x1, local copies, waits for them, and re-layouts  1.87 us

profile of v5, /device:TPU:24, one launch (start us, length us, event | category | flops | bytes accessed | tf_op | source)
XLA Modules:
  0.0 55.9 jit_solution(2453405071319750880)
XLA Ops:
  0.0 54.0 %shard_map.64 = f32[256,512]{1,0:T(8,128)} custom-call(s32[16,32]{1,0:T(8,128)} %ids_ref.1, s32[16]{0:T(128)} %counts_ref.1, s32[16,16]{1,0:T(8,128)} %pattern_ref.1, s32[16,32]{1,0:T(8,128)} %ids_ref.1, f32[64,128]{1,0:T(8,128)} %var_ref.1, bf16[2,8,128,128]{3,2,1,0:T(8,128)(2,1)} %source_ref.1, f32[256,512]{1,0:T(8,128)} %prior_source.1), custom_call_target="tpu_custom_call" | custom-call | tf_op jit(solution)/shard_map/pallas_call | solution.py:319
  54.0 1.9 %copy.8 = f32[256,512]{1,0:T(8,128)} copy(f32[256,512]{1,0:T(8,128)} %shard_map.64) | data formatting | bytes 1048576

commit v6 on v5

--- a/solution.py
+++ b/solution.py
@@ -10,10 +10,10 @@
 MESH = pl.DeviceIdType.MESH
 
 
-def kernel(planes, fold, obs_ref, counts_ref, pattern_ref, ids_ref, var_ref, source_ref, prior_source, out_ref,
-           panels_ref, prior_ref, table, place_ref, weights, leaving, held, turned, rows, cols, total, inbox,
+def kernel(planes, fold, source_ref, obs_source, counts_source, var_source, pattern_source, prior_source, out_ref,
+           obs_ref, counts_ref, pattern_ref, ids_ref, var_ref, panels_ref, prior_ref, table, place_ref, weights, leaving, held, turned, rows, cols, total, inbox,
            y_send, y_recv, z_send, z_recv, x_send, x_recv, r_send, r_recv, n_send, n_recv,
-           t_send, t_recv, keep, fetch, prior_fetch, place_fetch):
+           t_send, t_recv, keep, fetch, place_fetch):
     row, col = lax.axis_index("row"), lax.axis_index("col")
     plane, part = row // fold, row % fold
     groups, share, size = panels_ref.shape[0], panels_ref.shape[1], panels_ref.shape[2]
@@ -35,10 +35,11 @@
     def other_part(step):
         return lax.rem(part + step, fold)
 
-    fetched = pltpu.make_async_copy(source_ref, panels_ref, fetch)
-    fetched.start()
-    prior_fetched = pltpu.make_async_copy(prior_source, prior_ref, prior_fetch)
-    prior_fetched.start()
+    fetches = [pltpu.make_async_copy(source, target, fetch.at[index]) for index, (source, target) in enumerate((
+        (obs_source, obs_ref), (counts_source, counts_ref), (var_source, var_ref), (source_ref, panels_ref),
+        (obs_source, ids_ref), (pattern_source, pattern_ref), (prior_source, prior_ref)))]
+    for fetched in fetches:
+        fetched.start()
     partners = [at(other_plane(s) * fold + part, col) for s in (1, planes - 1)]
     partners += [at(row, other_col(s)) for s in range(1, planes)]
     partners += [at(plane * fold + other_part(s), col) for s in range(1, fold)]
@@ -46,6 +47,8 @@
     for partner in partners:
         pl.semaphore_signal(barrier, inc=1, device_id=partner, device_id_type=MESH)
 
+    for fetched in fetches[:3]:
+        fetched.wait()
     factors = []
     for g in range(groups):
         block = row * groups + g
@@ -54,7 +57,7 @@
             live = jnp.where(slot < counts_ref[block], 1.0, 0.0)
             factors.append(jnp.sqrt(var_ref[pl.ds(obs_ref[block, slot], 1), :]) * live)
     weights[...] = jnp.concatenate(factors, axis=0).T
-    fetched.wait()
+    fetches[3].wait()
 
     def scaled(to_part, g, p):
         j = g * share + p
@@ -81,11 +84,11 @@
         return pl.ds(slot_col * share, share)
 
     def x_copy(to_col, order, g, landing):
-        return copy(held.at[to_col, other_part(order), g], cols[order].at[g, slots_of(landing)],
+        return copy(held.at[to_col, other_part(order), g], cols[order * groups + g].at[slots_of(landing)],
                     x_send.at[to_col, order, g], x_recv.at[landing, order, g], at(row, to_col))
 
     def keep_copy(order, g):
-        return pltpu.make_async_copy(held.at[col, other_part(order), g], cols[order].at[g, slots_of(col)],
+        return pltpu.make_async_copy(held.at[col, other_part(order), g], cols[order * groups + g].at[slots_of(col)],
                                      keep.at[order, g])
 
     def far_copy(step, landing):
@@ -95,9 +98,9 @@
         source = turned if index == 0 else rows.at[slot]
         return copy(source, rows.at[landing], n_send.at[index], n_recv.at[index], at(row, near))
 
-    def t_copy(step, chunk, g):
-        return copy(total.at[other_part(step), chunk, g], inbox.at[step - 1, chunk, g],
-                    t_send.at[step - 1, chunk, g], t_recv.at[step - 1, chunk, g],
+    def t_copy(step, chunk, h, g):
+        return copy(total.at[other_part(step), chunk, h, g], inbox.at[step - 1, chunk, h, g],
+                    t_send.at[step - 1, chunk, h, g], t_recv.at[step - 1, chunk, h, g],
                     at(plane * fold + other_part(step), col))
 
     def spread(from_plane, order, g):
@@ -144,16 +147,16 @@
             spread(plane, step, g)
             turn(other_part(step), g)
     ids = lax.broadcasted_iota(jnp.int32, table.shape, 1)
+    fetches[4].wait()
     found = jnp.full(table.shape, slot_count, jnp.int32)
     for p in range(slot_count):
         found = jnp.where(ids_ref[:, p:p + 1] == ids, p, found)
     table[...] = found
     placed = pltpu.make_async_copy(table, place_ref, place_fetch)
     placed.start()
-    for order in range(fold):
-        for h in range(groups):
-            cols[order][h, slot_count] = jnp.zeros((depth, size), jnp.bfloat16)
-    own_row = pltpu.make_async_copy(turned, rows.at[col], fetch)
+    for piece in range(fold * groups):
+        cols[piece][slot_count] = jnp.zeros((depth, size), jnp.bfloat16)
+    own_row = pltpu.make_async_copy(turned, rows.at[col], fetch.at[len(fetches)])
     own_row.start()
     near_copy(col, 0, col).start()
     for step in far_steps:
@@ -168,28 +171,25 @@
     block_cols = groups * fold
     paired = 2 if planes % 2 == 0 else 1
 
-    def partial_tiles(step_part, order):
-        row_part, chunk = other_part(step_part), other_part(order)
-        first = col * block_cols + chunk * groups
-        for g in range(groups):
-            a = (plane * fold + row_part) * groups + g
-
-            def step(i, unused):
-                for slot_col in [i * paired + k for k in range(paired)]:
-                    lines = []
-                    for p in range(share):
-                        obs = obs_ref[a, slot_col * share + p]
-                        lines.append(jnp.concatenate(
-                            [cols[order][h, place_ref[first + h, obs]] for h in range(groups)], axis=1))
-                    total[row_part, chunk, g] += jnp.dot(
+    def partial_tiles(step_part, piece):
+        row_part, chunk, h = other_part(step_part), other_part(piece // groups), piece % groups
+        b = col * block_cols + chunk * groups + h
+
+        def step(i, unused):
+            for slot_col in [i * paired + k for k in range(paired)]:
+                for g in range(groups):
+                    a = (plane * fold + row_part) * groups + g
+                    lines = [cols[piece][place_ref[b, obs_ref[a, slot_col * share + p]]] for p in range(share)]
+                    total[row_part, chunk, h, g] += jnp.dot(
                         rows[slot_col, row_part, g], jnp.concatenate(lines, axis=0),
                         preferred_element_type=jnp.float32)
-                return unused
-
-            total[row_part, chunk, g] = jnp.zeros(total.shape[3:], jnp.float32)
-            lax.fori_loop(0, planes // paired, step, 0)
-            if step_part > 0:
-                t_copy(step_part, chunk, g).start()
+            return unused
+
+        total[row_part, chunk, h] = jnp.zeros(total.shape[3:], jnp.float32)
+        lax.fori_loop(0, planes // paired, step, 0)
+        if step_part > 0:
+            for g in range(groups):
+                t_copy(step_part, chunk, h, g).start()
 
     def await_rows():
         placed.wait()
@@ -199,28 +199,26 @@
             slot = lax.rem(near + step, planes)
             near_copy(slot, index + 1, slot).wait_recv()
 
-    def await_columns(order):
-        for g in range(groups):
-            keep_copy(order, g).wait()
-            for step in range(1, planes):
-                x_copy(col, order, g, other_col(step)).wait_recv()
+    def await_columns(piece):
+        order, g = piece // groups, piece % groups
+        keep_copy(order, g).wait()
+        for step in range(1, planes):
+            x_copy(col, order, g, other_col(step)).wait_recv()
 
     distance = jnp.maximum(plane - col, col - plane)
-    units = [(step, order) for step in range(1, fold) for order in range(fold)]
-    units += [(0, order) for order in range(fold)]
-
-    def products_between(piece):
-        pieces = fold * groups
-        mine = units[piece * len(units) // pieces:(piece + 1) * len(units) // pieces]
-        if not mine:
-            return
+    pieces = fold * groups
+    units = [(step, piece) for step in range(1, fold) for piece in range(pieces)]
+    units += [(0, piece) for piece in range(pieces)]
+
+    def products_between(turn_at):
+        mine = units[turn_at * len(units) // pieces:(turn_at + 1) * len(units) // pieces]
 
         @pl.when(distance < planes - 1)
         def _():
-            if mine[0] == units[0]:
+            if turn_at == 0:
                 await_rows()
             for unit in mine:
-                if unit in units[:fold]:
+                if unit in units[:pieces]:
                     await_columns(unit[1])
                 partial_tiles(*unit)
 
@@ -257,33 +255,33 @@
     @pl.when(distance == planes - 1)
     def _():
         await_rows()
-        for order in range(fold):
-            await_columns(order)
+        for piece in range(pieces):
+            await_columns(piece)
             for step in range(1, fold):
-                partial_tiles(step, order)
-            partial_tiles(0, order)
-
-    prior_fetched.wait()
-    for order in range(fold):
-        chunk = other_part(order)
-        for g in range(groups):
-            update = total[part, chunk, g]
+                partial_tiles(step, piece)
+            partial_tiles(0, piece)
+
+    for fetched in fetches[5:]:
+        fetched.wait()
+    for piece in range(pieces):
+        chunk, h = other_part(piece // groups), piece % groups
+        for g in range(groups):
+            update = total[part, chunk, h, g]
             for step in range(1, fold):
-                t_copy(step, chunk, g).wait_recv()
-                update = update + inbox[step - 1, chunk, g]
-            for h in range(groups):
-                a, b = row * groups + g, col * block_cols + chunk * groups + h
-                kept = pattern_ref[jnp.minimum(a, b), jnp.maximum(a, b)] == 1
-                down = pl.ds(pl.multiple_of((chunk * groups + h) * size, size), size)
-                across = slice(g * size, (g + 1) * size)
-                out_ref[across, down] = prior_ref[across, down] + jnp.where(
-                    kept, update[:, h * size:(h + 1) * size], jnp.zeros((size, size), jnp.float32))
+                t_copy(step, chunk, h, g).wait_recv()
+                update = update + inbox[step - 1, chunk, h, g]
+            a, b = row * groups + g, col * block_cols + chunk * groups + h
+            kept = pattern_ref[jnp.minimum(a, b), jnp.maximum(a, b)] == 1
+            across = slice(g * size, (g + 1) * size)
+            down = pl.ds(pl.multiple_of((chunk * groups + h) * size, size), size)
+            out_ref[across, down] = prior_ref[across, down] + jnp.where(kept, update, jnp.zeros_like(update))
 
     for step in range(1, fold):
         for g in range(groups):
             y_copy(step, g, part).wait_send()
             for chunk in range(fold):
-                t_copy(step, chunk, g).wait_send()
+                for h in range(groups):
+                    t_copy(step, chunk, h, g).wait_send()
     for index in range(planes // 2):
         near_copy(col, index, col).wait_send()
     for step in far_steps:
@@ -308,20 +306,23 @@
     groups, share, size, _ = panels.shape
     depth = size // fold
     names = -(-inv_var.shape[0] // 128) * 128
-    smem = pl.BlockSpec(memory_space=pltpu.SMEM)
-    vmem = pl.BlockSpec(memory_space=pltpu.VMEM)
-    anywhere = pl.BlockSpec(memory_space=pl.ANY)
+    far_memory = pl.BlockSpec(memory_space=pltpu.HBM)
     dma = pltpu.SemaphoreType.DMA
     others = max(fold - 1, 1)
     panel = (fold, groups, share, depth, size)
     turned = (fold, groups, size, share * depth)
-    tile = (fold, groups, size, groups * size)
+    tile = (fold, groups, groups, size, size)
     return pl.pallas_call(
         functools.partial(kernel, planes, fold),
         out_shape=jax.ShapeDtypeStruct(prior.shape, prior.dtype),
-        in_specs=[smem, smem, smem, vmem, vmem, anywhere, anywhere],
-        out_specs=vmem,
+        in_specs=[far_memory] * 6,
+        out_specs=pl.BlockSpec(memory_space=pltpu.VMEM),
         scratch_shapes=[
+            pltpu.SMEM(obs_of.shape, jnp.int32),
+            pltpu.SMEM(counts.shape, jnp.int32),
+            pltpu.SMEM(pattern.shape, jnp.int32),
+            pltpu.VMEM(obs_of.shape, jnp.int32),
+            pltpu.VMEM(inv_var.shape, jnp.float32),
             pltpu.VMEM(panels.shape, jnp.bfloat16),
             pltpu.VMEM(prior.shape, jnp.float32),
             pltpu.VMEM((obs_of.shape[0], names), jnp.int32),
@@ -331,7 +332,7 @@
             pltpu.VMEM((planes,) + panel, jnp.bfloat16),
             pltpu.VMEM(turned, jnp.bfloat16),
             pltpu.VMEM((planes,) + turned, jnp.bfloat16),
-            (pltpu.VMEM((groups, obs_of.shape[1] + 1, depth, size), jnp.bfloat16),) * fold,
+            (pltpu.VMEM((obs_of.shape[1] + 1, depth, size), jnp.bfloat16),) * (fold * groups),
             pltpu.VMEM((fold,) + tile, jnp.float32),
             pltpu.VMEM((others,) + tile, jnp.float32),
             dma((others, groups)), dma((fold, groups)),
@@ -339,12 +340,12 @@
             dma((planes, fold, groups)), dma((planes, fold, groups)),
             dma((planes,)), dma((planes,)),
             dma((planes // 2,)), dma((planes // 2,)),
-            dma((others, fold, groups)), dma((others, fold, groups)),
-            dma((fold, groups)), dma, dma, dma,
+            dma((others, fold, groups, groups)), dma((others, fold, groups, groups)),
+            dma((fold, groups)), dma((8,)), dma,
         ],
         compiler_params=pltpu.CompilerParams(
             collective_id=0, has_side_effects=True, vmem_limit_bytes=60 * 1024 * 1024),
-    )(obs_of, counts, pattern, obs_of, inv_var, panels, prior)
+    )(panels, obs_of, counts, inv_var, pattern, prior)
 
 
 def solution(mesh):

time: 56.3 us -> 54 us (0.959)
  Pallas kernels: 54 us -> 51.9 us
    pallas_call x1, Pallas kernels: 54 us -> 51.9 us  [on_device(): pl.pallas_call(functools.partial(kernel, planes, fold), out_shape=jax.Sha...]
where the time goes in v6:
time: 54 us; the launch traced here: 53.7 us
  Pallas kernels  51.9 us (96%)
  local copies, waits for them, and re-layouts  1.87 us (3%)
    pallas_call x1, Pallas kernels, on_device(): pl.pallas_call(functools.partial(kernel, planes, fold), out_shape=jax.Sha...  51.9 us
    unnamed x1, local copies, waits for them, and re-layouts  1.87 us

profile of v6, /device:TPU:24, one launch (start us, length us, event | category | flops | bytes accessed | tf_op | source)
XLA Modules:
  0.0 53.7 jit_solution(13821107933575187852)
XLA Ops:
  0.0 51.9 %shard_map.64 = f32[256,512]{1,0:T(8,128)} custom-call(bf16[2,8,128,128]{3,2,1,0:T(8,128)(2,1)} %source_ref.1, s32[16,32]{1,0:T(8,128)} %obs_source.1, s32[16]{0:T(128)} %counts_source.1, f32[64,128]{1,0:T(8,128)} %var_source.1, s32[16,16]{1,0:T(8,128)} %pattern_source.1, f32[256,512]{1,0:T(8,128)} %prior_source.1), custom_call_target="tpu_custom_call" | custom-call | tf_op jit(solution)/shard_map/pallas_call | solution.py:315
  51.9 1.9 %copy.8 = f32[256,512]{1,0:T(8,128)} copy(f32[256,512]{1,0:T(8,128)} %shard_map.64) | data formatting | bytes 1048576

commit v7 on v6

--- a/solution.py
+++ b/solution.py
@@ -91,8 +91,9 @@
         return pltpu.make_async_copy(held.at[col, other_part(order), g], cols[order * groups + g].at[slots_of(col)],
                                      keep.at[order, g])
 
-    def far_copy(step, landing):
-        return copy(turned, rows.at[landing], r_send.at[step], r_recv.at[landing], at(row, other_col(step)))
+    def far_copy(step, chunk, landing):
+        return copy(turned.at[chunk], rows.at[landing, chunk], r_send.at[step, chunk],
+                    r_recv.at[landing, chunk], at(row, other_col(step)))
 
     def near_copy(slot, index, landing):
         source = turned if index == 0 else rows.at[slot]
@@ -139,6 +140,8 @@
     for g in range(groups):
         spread(plane, 0, g)
         turn(part, g)
+    for step in far_steps:
+        far_copy(step, part, col).start()
     for step in range(1, fold):
         for g in range(groups):
             y_copy(step, g, other_part(step)).wait_recv()
@@ -146,6 +149,8 @@
         for g in range(groups):
             spread(plane, step, g)
             turn(other_part(step), g)
+        for far in far_steps:
+            far_copy(far, other_part(step), col).start()
     ids = lax.broadcasted_iota(jnp.int32, table.shape, 1)
     fetches[4].wait()
     found = jnp.full(table.shape, slot_count, jnp.int32)
@@ -159,13 +164,12 @@
     own_row = pltpu.make_async_copy(turned, rows.at[col], fetch.at[len(fetches)])
     own_row.start()
     near_copy(col, 0, col).start()
-    for step in far_steps:
-        far_copy(step, col).start()
 
     def pass_rows():
         for index, step in enumerate(far_steps):
             slot = other_col(step)
-            far_copy(step, slot).wait_recv()
+            for chunk in range(fold):
+                far_copy(step, chunk, slot).wait_recv()
             near_copy(slot, index + 1, slot).start()
 
     block_cols = groups * fold
@@ -207,20 +211,24 @@
 
     distance = jnp.maximum(plane - col, col - plane)
     pieces = fold * groups
-    units = [(step, piece) for step in range(1, fold) for piece in range(pieces)]
-    units += [(0, piece) for piece in range(pieces)]
-
-    def products_between(turn_at):
-        mine = units[turn_at * len(units) // pieces:(turn_at + 1) * len(units) // pieces]
-
+
+    def products(piece):
+        if piece == 0:
+            await_rows()
+        await_columns(piece)
+        for step_part in range(1, fold):
+            partial_tiles(step_part, piece)
+        partial_tiles(0, piece)
+
+    def products_between(piece):
         @pl.when(distance < planes - 1)
         def _():
-            if turn_at == 0:
-                await_rows()
-            for unit in mine:
-                if unit in units[:pieces]:
-                    await_columns(unit[1])
-                partial_tiles(*unit)
+            products(piece)
+
+        if piece > 0:
+            @pl.when(distance == planes - 1)
+            def _():
+                products(piece - 1)
 
     for step in range(1, planes):
         below, above = plane - step, plane + step
@@ -254,12 +262,7 @@
 
     @pl.when(distance == planes - 1)
     def _():
-        await_rows()
-        for piece in range(pieces):
-            await_columns(piece)
-            for step in range(1, fold):
-                partial_tiles(step, piece)
-            partial_tiles(0, piece)
+        products(pieces - 1)
 
     for fetched in fetches[5:]:
         fetched.wait()
@@ -285,7 +288,8 @@
     for index in range(planes // 2):
         near_copy(col, index, col).wait_send()
     for step in far_steps:
-        far_copy(step, col).wait_send()
+        for chunk in range(fold):
+            far_copy(step, chunk, col).wait_send()
     for chunk in range(fold):
         for g in range(groups):
             for step in range(1, planes):
@@ -338,7 +342,7 @@
             dma((others, groups)), dma((fold, groups)),
             dma((2, planes, fold, groups)), dma((planes, fold, groups)),
             dma((planes, fold, groups)), dma((planes, fold, groups)),
-            dma((planes,)), dma((planes,)),
+            dma((planes, fold)), dma((planes, fold)),
             dma((planes // 2,)), dma((planes // 2,)),
             dma((others, fold, groups, groups)), dma((others, fold, groups, groups)),
             dma((fold, groups)), dma((8,)), dma,

time: 54 us -> 54 us (level)
  no operation moved by 1% of the time
where the time goes in v7:
time: 54 us; the launch traced here: 53.8 us
  Pallas kernels  51.9 us (96%)
  local copies, waits for them, and re-layouts  1.87 us (3%)
    pallas_call x1, Pallas kernels, on_device(): pl.pallas_call(functools.partial(kernel, planes, fold), out_shape=jax.Sha...  51.9 us
    unnamed x1, local copies, waits for them, and re-layouts  1.87 us

profile of v7, /device:TPU:24, one launch (start us, length us, event | category | flops | bytes accessed | tf_op | source)
XLA Modules:
  0.0 53.8 jit_solution(742881716760067990)
XLA Ops:
  0.0 51.9 %shard_map.64 = f32[256,512]{1,0:T(8,128)} custom-call(bf16[2,8,128,128]{3,2,1,0:T(8,128)(2,1)} %source_ref.1, s32[16,32]{1,0:T(8,128)} %obs_source.1, s32[16]{0:T(128)} %counts_source.1, f32[64,128]{1,0:T(8,128)} %var_source.1, s32[16,16]{1,0:T(8,128)} %pattern_source.1, f32[256,512]{1,0:T(8,128)} %prior_source.1), custom_call_target="tpu_custom_call" | custom-call | tf_op jit(solution)/shard_map/pallas_call | solution.py:319
  51.9 1.9 %copy.8 = f32[256,512]{1,0:T(8,128)} copy(f32[256,512]{1,0:T(8,128)} %shard_map.64) | data formatting | bytes 1048576

commit v8 on v7

--- a/solution.py
+++ b/solution.py
@@ -212,13 +212,20 @@
     distance = jnp.maximum(plane - col, col - plane)
     pieces = fold * groups
 
+    at_end = (plane == 0) | (plane == planes - 1)
+    own_later = at_end & (distance < planes - 1)
+    own_now = jnp.logical_not(own_later)
+
     def products(piece):
         if piece == 0:
             await_rows()
         await_columns(piece)
         for step_part in range(1, fold):
             partial_tiles(step_part, piece)
-        partial_tiles(0, piece)
+
+        @pl.when(own_now)
+        def _():
+            partial_tiles(0, piece)
 
     def products_between(piece):
         @pl.when(distance < planes - 1)
@@ -263,6 +270,11 @@
     @pl.when(distance == planes - 1)
     def _():
         products(pieces - 1)
+
+    @pl.when(own_later)
+    def _():
+        for piece in range(pieces):
+            partial_tiles(0, piece)
 
     for fetched in fetches[5:]:
         fetched.wait()

time: 54 us -> 54 us (level)
  no operation moved by 1% of the time
where the time goes in v8:
time: 54 us; the launch traced here: 53.8 us
  Pallas kernels  51.9 us (96%)
  local copies, waits for them, and re-layouts  1.87 us (3%)
    pallas_call x1, Pallas kernels, on_device(): pl.pallas_call(functools.partial(kernel, planes, fold), out_shape=jax.Sha...  51.9 us
    unnamed x1, local copies, waits for them, and re-layouts  1.87 us

profile of v8, /device:TPU:24, one launch (start us, length us, event | category | flops | bytes accessed | tf_op | source)
XLA Modules:
  0.0 53.8 jit_solution(12329497702469747438)
XLA Ops:
  0.0 51.9 %shard_map.64 = f32[256,512]{1,0:T(8,128)} custom-call(bf16[2,8,128,128]{3,2,1,0:T(8,128)(2,1)} %source_ref.1, s32[16,32]{1,0:T(8,128)} %obs_source.1, s32[16]{0:T(128)} %counts_source.1, f32[64,128]{1,0:T(8,128)} %var_source.1, s32[16,16]{1,0:T(8,128)} %pattern_source.1, f32[256,512]{1,0:T(8,128)} %prior_source.1), custom_call_target="tpu_custom_call" | custom-call | tf_op jit(solution)/shard_map/pallas_call | solution.py:331
  51.9 1.9 %copy.8 = f32[256,512]{1,0:T(8,128)} copy(f32[256,512]{1,0:T(8,128)} %shard_map.64) | data formatting | bytes 1048576

commit v9 on v7

--- a/solution.py
+++ b/solution.py
@@ -257,7 +257,7 @@
 
                 if step == planes - 1:
                     products_between(order * groups + g)
-                elif step == planes - 2 and order * groups + g == min(1, fold * groups - 1):
+                elif step == planes - 2 and order * groups + g == fold * groups - 1:
                     pass_rows()
 
     @pl.when(distance == planes - 1)

time: 54 us -> 51.9 us (0.961); the launches traced: 53.8 us -> 51 us
  Pallas kernels: 51.9 us -> 49.1 us
    pallas_call x1, Pallas kernels: 51.9 us -> 49.1 us  [on_device(): pl.pallas_call(functools.partial(kernel, planes, fold), out_shape=jax.Sha...]
where the time goes in v9:
time: 51.9 us; the launch traced here: 51 us
  Pallas kernels  49.1 us (95%)
  local copies, waits for them, and re-layouts  1.87 us (4%)
    pallas_call x1, Pallas kernels, on_device(): pl.pallas_call(functools.partial(kernel, planes, fold), out_shape=jax.Sha...  49.1 us
    unnamed x1, local copies, waits for them, and re-layouts  1.87 us

profile of v9, /device:TPU:24, one launch (start us, length us, event | category | flops | bytes accessed | tf_op | source)
XLA Modules:
  0.0 51.0 jit_solution(1478144769515076802)
XLA Ops:
  0.0 49.1 %shard_map.64 = f32[256,512]{1,0:T(8,128)} custom-call(bf16[2,8,128,128]{3,2,1,0:T(8,128)(2,1)} %source_ref.1, s32[16,32]{1,0:T(8,128)} %obs_source.1, s32[16]{0:T(128)} %counts_source.1, f32[64,128]{1,0:T(8,128)} %var_source.1, s32[16,16]{1,0:T(8,128)} %pattern_source.1, f32[256,512]{1,0:T(8,128)} %prior_source.1), custom_call_target="tpu_custom_call" | custom-call | tf_op jit(solution)/shard_map/pallas_call | solution.py:319
  49.1 1.9 %copy.8 = f32[256,512]{1,0:T(8,128)} copy(f32[256,512]{1,0:T(8,128)} %shard_map.64) | data formatting | bytes 1048576
